TPU v7x, 32 devices: a whole 2x2x4 slice. The times are simulated.
32 devices in a mesh: row: 8 (over y, x, core), col: 4 (over z).
Axes of the slice: x: 2, y: 2, z: 4, core: 2. Of those that a mesh axis runs over, the one named last changes fastest.
Arguments:
- covariance: float32 [12288, 12288], P('row', 'col'), may hold values from -6 to 6
- east_wind: float32 [96, 128], replicated, may hold values from -0.3 to 0.3
- north_wind: float32 [96, 128], replicated, may hold values from -0.3 to 0.3
- diffuse_lon: float32 [96, 128], replicated, may hold values from 0.05 to 0.2
- diffuse_lat: float32 [96, 128], replicated, may hold values from 0.05 to 0.2
Outputs:
- propagated: float32 [12288, 12288], P('row', 'col')
All inputs are finite; a program needn't handle non-finite values.
Results may differ from a plain program's by a relative error of at most 0.00002.
Values sent between devices are 32-bit elements; how exact they have to be, the bound alone decides.
A program may use at most 192 MiB of HBM per device.

v0:
```python
import functools

import jax
import jax.numpy as jnp
from jax import lax
from jax.experimental import pallas as pl
from jax.experimental.pallas import tpu as pltpu
from jax.sharding import PartitionSpec as P

NLON = 128
STEPS = 3
UNIT = STEPS * NLON
WIDE = 256
BLOCK = 192
VMEM = 52 * 1024 * 1024


OFFSETS = [(y, x) for y in range(-STEPS, STEPS + 1) for x in range(-STEPS + abs(y), STEPS + 1 - abs(y))]


def power_kernel(east_wind, north_wind, diffuse_lon, diffuse_lat, plain, rolled):
    lon, lat = diffuse_lon[...], diffuse_lat[...]
    half_east, half_north = 0.5 * east_wind[...], 0.5 * north_wind[...]
    one = {
        (0, 0): 1.0 - 2.0 * lon - 2.0 * lat,
        (0, 1): lon - half_east,
        (0, -1): lon + half_east,
        (1, 0): lat - half_north,
        (-1, 0): lat + half_north,
    }
    lines = lon.shape[0]
    line = lax.broadcasted_iota(jnp.int32, lon.shape, 0)

    def seen(field, y, x):
        if x:
            return pltpu.roll(field, -x % NLON, 1)
        if y:
            edge = lines - 1 if y > 0 else 0
            return jnp.where(line == edge, 0.0, pltpu.roll(field, -y % lines, 0))
        return field

    power = dict(one)
    for _ in range(STEPS - 1):
        made = {}
        for (y, x), field in power.items():
            for (sy, sx), scale in one.items():
                term = scale * seen(field, sy, sx)
                at = (y + sy, x + sx)
                made[at] = made[at] + term if at in made else term
        power = made
    for k, (y, x) in enumerate(OFFSETS):
        plain[k] = power[y, x]
        rolled[k] = pltpu.roll(power[y, x], x % NLON, 1)


def powers(tables):
    shape = jax.ShapeDtypeStruct((len(OFFSETS),) + tables[0].shape, jnp.float32)
    return pl.pallas_call(
        power_kernel,
        out_shape=(shape, shape),
        compiler_params=pltpu.CompilerParams(vmem_limit_bytes=VMEM),
        cost_estimate=pl.CostEstimate(flops=10**7, bytes_accessed=10**7, transcendentals=0),
    )(*tables)


def split(value):
    high = value.astype(jnp.bfloat16)
    return high, (value - high.astype(jnp.float32)).astype(jnp.bfloat16)


def block_kernel(made, transposed, offset, table, out):
    base = offset[0] + pl.program_id(0) * made
    sub = lax.broadcasted_iota(jnp.int32, (NLON, NLON), 0)
    lane = lax.broadcasted_iota(jnp.int32, (NLON, NLON), 1)
    away = (sub - lane if transposed else lane - sub) & (NLON - 1)
    read = made + 2 * STEPS
    for a in range(made):
        for b in range(read):
            y = b - a - STEPS
            value = jnp.zeros((NLON, NLON), jnp.float32)
            for k, (oy, x) in enumerate(OFFSETS):
                if oy == y:
                    line = table[k, pl.ds(base + a, 1), :]
                    value = jnp.where(away == x % NLON, jnp.broadcast_to(line, (NLON, NLON)), value)
            high, low = split(value)
            mine, theirs = slice(a * NLON, (a + 1) * NLON), slice(b * NLON, (b + 1) * NLON)
            if transposed:
                out[0, theirs, mine] = high
                out[0, slice((read + b) * NLON, (read + b + 1) * NLON), mine] = low
            else:
                out[0, mine, theirs] = high
                out[0, slice((made + a) * NLON, (made + a + 1) * NLON), theirs] = low


def blocks_of(table, offset, groups, made, transposed):
    read = made + 2 * STEPS
    shape = (2 * read * NLON, made * NLON) if transposed else (2 * made * NLON, read * NLON)
    return pl.pallas_call(
        functools.partial(block_kernel, made, transposed),
        grid=(groups,),
        in_specs=[
            pl.BlockSpec(memory_space=pltpu.SMEM),
            pl.BlockSpec(table.shape, lambda i: (0, 0, 0)),
        ],
        out_specs=pl.BlockSpec((1,) + shape, lambda i: (i, 0, 0)),
        out_shape=jax.ShapeDtypeStruct((groups,) + shape, jnp.bfloat16),
        compiler_params=pltpu.CompilerParams(vmem_limit_bytes=VMEM),
        cost_estimate=pl.CostEstimate(flops=10**7, bytes_accessed=2 * 10**7, transcendentals=0),
    )(offset.reshape(1).astype(jnp.int32), table)


def dot(a, b):
    return jnp.dot(a, b, preferred_element_type=jnp.float32)


def stencil(c, east, west, north, south, coef):
    return coef[0] * c + coef[1] * east + coef[2] * west + coef[3] * north + coef[4] * south


def column_kernel(parts, sides, *refs):
    ins, tables, out = refs[: len(parts)], refs[len(parts)], refs[-1]
    for side, (names, first, count) in enumerate(sides):

        def source(line):
            part, at = divmod(line, STEPS)
            return ins[names[part]][at * NLON : (at + 1) * NLON, :]

        lines = count + 2 * STEPS
        got = {}
        for line in range(lines):
            got[0, line] = source(line)
            for step in range(1, STEPS + 1):
                mid = line - step
                if mid < step:
                    continue
                c = got[step - 1, mid]
                row = first + mid - 1
                value = stencil(
                    c,
                    pltpu.roll(c, NLON - 1, 0),
                    pltpu.roll(c, 1, 0),
                    got[step - 1, mid + 1],
                    got[step - 1, mid - 1],
                    [tables[k, row] for k in range(5)],
                )
                got.pop((step - 1, mid - 1))
                if step < STEPS:
                    got[step, mid] = value
                else:
                    at = sum(s[2] for s in sides[:side]) + mid - STEPS
                    out[at * NLON : (at + 1) * NLON, :] = value


def column_sweep(arrays, sides, width, coefs):
    total = sum(count for _, _, count in sides) * NLON
    in_specs = [
        pl.BlockSpec((UNIT, NLON), functools.partial(lambda i, r, c, skip: (r, jnp.where(i < UNIT // NLON, i + c, i + c + skip)), r=r, c=c, skip=skip)) for _, r, c, skip in arrays
    ]
    in_specs.append(pl.BlockSpec(coefs.shape, lambda i: (0, 0, 0, 0)))
    work = total * width
    return pl.pallas_call(
        functools.partial(column_kernel, arrays, sides),
        grid=(width // NLON,),
        in_specs=in_specs,
        out_specs=pl.BlockSpec((total, NLON), lambda i: (0, i)),
        out_shape=jax.ShapeDtypeStruct((total, width), jnp.float32),
        compiler_params=pltpu.CompilerParams(vmem_limit_bytes=VMEM),
        cost_estimate=pl.CostEstimate(flops=work * 40, bytes_accessed=work * 12, transcendentals=0),
    )(*[a[0] for a in arrays], coefs)


def row_kernel(count, *refs):
    ins, tables, out, both = refs[: count + 2], refs[count + 2], refs[-2], refs[-1]
    rows = out.shape[0]
    read = (2 + 2 * STEPS) * NLON
    for n, ref in enumerate(ins):
        cols = slice(n * UNIT, (n + 1) * UNIT)
        both[:rows, cols], both[rows:, cols] = split(ref[...])
    for pair in range(count * STEPS // 2):
        cols = slice(pair * 2 * NLON, pair * 2 * NLON + read)
        first = dot(both[:, cols], tables[pair, :read, :])
        other = dot(both[:rows, cols], tables[pair, read:, :])
        out[:, pair * 2 * NLON : (pair + 1) * 2 * NLON] = first[:rows] + (first[rows:] + other)


def row_sweep(arrays, part, tables, out_rows, row_block, out_cols, col_block, buffer):
    count = len(arrays) - 2
    rows = arrays[0][0].shape[0]
    pairs = count * STEPS // 2
    in_specs = [pl.BlockSpec((BLOCK, UNIT), functools.partial(lambda i, c: (i, c), c=c)) for _, c in arrays]
    in_specs.append(
        pl.BlockSpec((pairs,) + tables.shape[1:], lambda i: (part, 0, 0), pipeline_mode=pl.Buffered(1))
    )
    operands = [a for a, _ in arrays] + [tables]
    aliases = {}
    if buffer is not None:
        in_specs.append(pl.BlockSpec(memory_space=pl.ANY))
        operands.append(buffer)
        aliases = {len(operands) - 1: 0}
    work = rows * count * UNIT
    return pl.pallas_call(
        functools.partial(row_kernel, count),
        grid=(rows // BLOCK,),
        in_specs=in_specs,
        out_specs=pl.BlockSpec((BLOCK, count * UNIT), lambda i: (row_block(i), col_block)),
        out_shape=jax.ShapeDtypeStruct((out_rows, out_cols), jnp.float32),
        input_output_aliases=aliases,
        scratch_shapes=[pltpu.VMEM((2 * BLOCK, len(arrays) * UNIT), jnp.bfloat16)],
        compiler_params=pltpu.CompilerParams(vmem_limit_bytes=VMEM),
        cost_estimate=pl.CostEstimate(flops=work * 40, bytes_accessed=work * 12, transcendentals=0),
    )(*operands)


def exchange(first, last, axis):
    devices = lax.axis_size(axis)
    up = [(i, i + 1) for i in range(devices - 1)]
    down = [(j, i) for i, j in up]
    return lax.ppermute(last, axis, up), lax.ppermute(first, axis, down)


def coefficients(tables, offset, lines):
    east_wind, north_wind, diffuse_lon, diffuse_lat = tables
    made = jnp.stack(
        [
            1.0 - 2.0 * diffuse_lon - 2.0 * diffuse_lat,
            diffuse_lon - 0.5 * east_wind,
            diffuse_lon + 0.5 * east_wind,
            diffuse_lat - 0.5 * north_wind,
            diffuse_lat + 0.5 * north_wind,
        ]
    )
    edge = STEPS - 1
    made = jnp.pad(made, ((0, 0), (edge, edge), (0, 0)))
    return lax.dynamic_slice_in_dim(made, offset, lines + 2 * edge, 1)


def body(covariance, east_wind, north_wind, diffuse_lon, diffuse_lat):
    tables = (east_wind, north_wind, diffuse_lon, diffuse_lat)
    rows, cols = covariance.shape
    row_lines, col_lines = rows // NLON, cols // NLON
    row_units, col_units = rows // UNIT, cols // UNIT
    row_coefs = coefficients(tables, lax.axis_index("row") * row_lines, row_lines)
    row_coefs = jnp.broadcast_to(row_coefs[:, :, :, None], row_coefs.shape + (NLON,))
    plain, _ = powers(tables)
    col_tables = blocks_of(plain, lax.axis_index("col") * col_lines, col_lines // 2, 2, True)

    if col_units == 1:
        pieces = [[0]]
    else:
        pieces = [[0, col_units - 1]]
        half = col_units // 2
        if col_units % 2 == 0 and col_units >= 6:
            pieces += [list(range(1, half + 1)), list(range(half + 1, col_units - 1))]
        elif col_units > 2:
            pieces += [list(range(1, col_units - 1))]

    def columns(units, low, high):
        parts = []
        for u in units:
            if parts and parts[-1][1] == u:
                parts[-1][1] = u + 1
            else:
                parts.append([u, u + 1])
        return jnp.concatenate([covariance[low:high, a * UNIT : b * UNIT] for a, b in parts], axis=1)

    halos = [exchange(columns(p, 0, UNIT), columns(p, rows - UNIT, rows), "row") for p in pieces]

    inner = None
    if row_units > 2:
        inner = column_sweep(
            [(covariance, r, 0, 0) for r in range(row_units)],
            [(list(range(row_units)), STEPS, row_lines - 2 * STEPS)],
            cols,
            row_coefs,
        )

    outer = []
    where = {}
    for k, (units, (before, after)) in enumerate(zip(pieces, halos)):
        width = len(units) * UNIT
        skip = (cols - 2 * UNIT) // NLON if k == 0 and col_units > 1 else 0
        blocks = [(covariance, r, units[0] * (UNIT // NLON), skip) for r in range(row_units)]
        if row_units == 1:
            arrays = [(before, 0, 0, 0), blocks[0], (after, 0, 0, 0)]
            sides = [([0, 1, 2], 0, STEPS)]
        else:
            arrays = [(before, 0, 0, 0), blocks[0], blocks[1], blocks[-2], blocks[-1], (after, 0, 0, 0)]
            sides = [([0, 1, 2], 0, STEPS), ([3, 4, 5], row_lines - STEPS, STEPS)]
        outer.append(column_sweep(arrays, sides, width, row_coefs))
        for at, u in enumerate(units):
            where[u] = (k, at)

    out_blocks, tiles = rows // BLOCK, UNIT // BLOCK
    halves = [list(range(col_units))]
    if len(pieces) == 3:
        halves = [list(range(half)), list(range(half, col_units))]

    edges = outer[0]
    outer_halo = exchange(edges[:, :UNIT], edges[:, -UNIT:], "col")
    out = None
    if inner is not None:
        inner_halo = exchange(inner[:, :UNIT], inner[:, cols - UNIT :], "col")
        arrays = [(inner_halo[0], 0)] + [(inner, u) for u in range(col_units)] + [(inner_halo[1], 0)]
        out = row_sweep(arrays, 0, col_tables, rows, lambda i: i + tiles, cols, 0, out)

    def outer_row(i):
        return jnp.where(i < tiles, i, i + out_blocks - 2 * tiles) if row_units > 1 else i

    for h, units in enumerate(halves):
        arrays = []
        for u in [units[0] - 1] + units + [units[-1] + 1]:
            if u < 0:
                arrays.append((outer_halo[0], 0))
            elif u == col_units:
                arrays.append((outer_halo[1], 0))
            else:
                arrays.append((outer[where[u][0]], where[u][1]))
        out = row_sweep(arrays, h, col_tables, rows, outer_row, cols, h, out)
    return out


def solution(mesh):
    return jax.shard_map(
        body,
        mesh=mesh,
        in_specs=(P("row", "col"), P(), P(), P(), P()),
        out_specs=P("row", "col"),
        check_vma=False,
    )
```

profile of v0, /device:TPU:1, one launch (start us, length us, event | category | flops | bytes accessed | tf_op | source)
XLA Modules:
  0.0 186.5 jit_solution(16058376735508066911)
XLA Ops:
  0.0 1.8 fusion
  1.8 1.1 pad_maximum_fusion
  2.9 4.5 %collective-permute-start.4 = (f32[384,768]{1,0:T(8,128)}, f32[384,768]{1,0:T(8,128)S(1)}, u32[]{:S(2)}, u32[]{:S(2)}) collective-permute-start(f32[384,768]{1,0:T(8,128)} %pad_maximum_fusion), channel_id=1, source_target_pairs={{0,4},{4,8},{8,12},{12,16},{16,20},{20,24},{24,28},{1,5},{5,9},{9,... | collective-permute-start | bytes 3538952 | tf_op jit(solution)/shard_map/ppermute | solution.py:218
  7.4 1.1 pad_maximum_fusion.1
  8.5 1.9 %collective-permute-start.5 = (f32[384,768]{1,0:T(8,128)}, f32[384,768]{1,0:T(8,128)}, u32[]{:S(2)}, u32[]{:S(2)}) collective-permute-start(f32[384,768]{1,0:T(8,128)} %pad_maximum_fusion.1), channel_id=1, source_target_pairs={{4,0},{8,4},{12,8},{16,12},{20,16},{24,20},{28,24},{5,1},{9,5},{13... | collective-permute-start | bytes 3538952 | tf_op jit(solution)/shard_map/ppermute | solution.py:218
  10.4 3.2 %fusion.1 = (f32[384,768]{1,0:T(8,128)}, f32[384,768]{1,0:T(8,128)}) fusion(f32[1536,3072]{1,0:T(8,128)} %refs_3_.7), kind=kLoop, calls=%fused_computation.9 | loop fusion | bytes 4718592 | tf_op jit(solution)/shard_map/slice | solution.py:264
  13.7 1.9 %collective-permute-start.3 = (f32[384,768]{1,0:T(8,128)}, f32[384,768]{1,0:T(8,128)}, u32[]{:S(2)}, u32[]{:S(2)}) collective-permute-start(f32[384,768]{1,0:T(8,128)} %get-tuple-element.11), channel_id=1, source_target_pairs={{4,0},{8,4},{12,8},{16,12},{20,16},{24,20},{28,24},{5,1},{9,5},{13... | collective-permute-start | bytes 3538952 | tf_op jit(solution)/shard_map/ppermute | solution.py:218
  15.6 3.8 %collective-permute-start.2 = (f32[384,768]{1,0:T(8,128)}, f32[384,768]{1,0:T(8,128)S(1)}, u32[]{:S(2)}, u32[]{:S(2)}) collective-permute-start(f32[384,768]{1,0:T(8,128)} %get-tuple-element.12), channel_id=1, source_target_pairs={{0,4},{4,8},{8,12},{12,16},{16,20},{20,24},{24,28},{1,5},{5,9},{9,... | collective-permute-start | bytes 3538952 | tf_op jit(solution)/shard_map/ppermute | solution.py:218
  19.4 4.8 %fusion.2 = (f32[384,1536]{1,0:T(8,128)}, f32[384,1536]{1,0:T(8,128)}) fusion(f32[1536,3072]{1,0:T(8,128)} %refs_3_.7), kind=kLoop, calls=%fused_computation.10 | loop fusion | bytes 9437184 | tf_op jit(solution)/shard_map/slice | solution.py:264
  24.2 1.9 %collective-permute-start.1 = (f32[384,1536]{1,0:T(8,128)}, f32[384,1536]{1,0:T(8,128)}, u32[]{:S(2)}, u32[]{:S(2)}) collective-permute-start(f32[384,1536]{1,0:T(8,128)} %get-tuple-element.13), channel_id=1, source_target_pairs={{4,0},{8,4},{12,8},{16,12},{20,16},{24,20},{28,24},{5,1},{9,5},{13... | collective-permute-start | bytes 7077896 | tf_op jit(solution)/shard_map/ppermute | solution.py:218
  26.3 3.1 %broadcast_in_dim.2.refs_6_.refs_4_ = f32[5,16,128,128]{3,2,1,0:T(8,128)} broadcast(f32[5,16,128]{2,1,0:T(8,128)S(1)} %pad_dynamic-slice_fusion), dimensions={0,1,2} | broadcast | bytes 5283840 | tf_op jit(solution)/shard_map/broadcast_in_dim | solution.py:243
  29.4 28.8 %shard_map.60.refs_1_.refs_2_.refs_3_.refs_4_.refs_5_.refs_6_.refs_7_.refs_8_ = f32[768,3072]{1,0:T(8,128)} custom-call(f32[1536,3072]{1,0:T(8,128)} %refs_3_.7, f32[1536,3072]{1,0:T(8,128)} %refs_3_.7, f32[1536,3072]{1,0:T(8,128)} %refs_3_.7, f32[1536,3072]{1,0:T(8,128)} %refs_3_.7, f32[5,16,128,128]{3,2,1,0:T(8,128)} %broadcast_in_dim.2.refs_6_.refs_4_), custom_call_target="tpu_custom_call" | custom-call | flops 94371840 | bytes 28311552 | tf_op jit(solution)/shard_map/pallas_call | solution.py:161
  58.1 3.6 %collective-permute-start = (f32[384,1536]{1,0:T(8,128)}, f32[384,1536]{1,0:T(8,128)}, u32[]{:S(2)}, u32[]{:S(2)}) collective-permute-start(f32[384,1536]{1,0:T(8,128)} %get-tuple-element.14), channel_id=1, source_target_pairs={{0,4},{4,8},{8,12},{12,16},{16,20},{20,24},{24,28},{1,5},{5,9},{9,... | collective-permute-start | bytes 7077896 | tf_op jit(solution)/shard_map/ppermute | solution.py:218
  61.8 2.8 %fusion.3 = (f32[768,384]{1,0:T(8,128)S(1)}, f32[768,384]{1,0:T(8,128)}) fusion(f32[768,3072]{1,0:T(8,128)} %shard_map.60.refs_1_.refs_2_.refs_3_.refs_4_.refs_5_.refs_6_.refs_7_.refs_8_), kind=kLoop, calls=%fused_computation.11 | loop fusion | bytes 4718592 | tf_op jit(solution)/shard_map/slice | solution.py:302
  64.6 1.3 collective-permute-start.9
  65.9 10.5 %shard_map.57.refs_1_.refs_4_ = f32[768,768]{1,0:T(8,128)} custom-call(f32[384,768]{1,0:T(8,128)S(1)} %collective-permute-done.4.refs_0_, f32[1536,3072]{1,0:T(8,128)} %refs_3_.7, f32[1536,3072]{1,0:T(8,128)} %refs_3_.7, f32[1536,3072]{1,0:T(8,128)} %refs_3_.7, f32[1536,3072]{1,0:T(8,128)} %refs_3_.7, f32[384,768]{1,0:T(8,128)} %collective-permute-done.5.refs_5_, ...), custom_call_target="tpu_custom_call" | custom-call | flops 23592960 | bytes 7077888 | tf_op jit(solution)/shard_map/pallas_call | solution.py:161
  76.3 5.0 %collective-permute-start.8 = (f32[768,384]{1,0:T(8,128)}, f32[768,384]{1,0:T(8,128)}, u32[]{:S(2)}, u32[]{:S(2)}) collective-permute-start(f32[768,384]{1,0:T(8,128)} %get-tuple-element.16), channel_id=1, source_target_pairs={{0,1},{1,2},{2,3},{4,5},{5,6},{6,7},{8,9},{9,10},{10,11},{12,13},{... | collective-permute-start | bytes 3538952 | tf_op jit(solution)/shard_map/ppermute | solution.py:218
  81.4 3.2 %fusion.4 = (f32[768,384]{1,0:T(8,128)}, f32[768,384]{1,0:T(8,128)}) fusion(f32[768,768]{1,0:T(8,128)} %shard_map.57.refs_1_.refs_4_), kind=kLoop, calls=%fused_computation.12 | loop fusion | bytes 4718592 | tf_op jit(solution)/shard_map/slice | solution.py:299
  84.6 2.2 %collective-permute-start.7 = (f32[768,384]{1,0:T(8,128)}, f32[768,384]{1,0:T(8,128)S(1)}, u32[]{:S(2)}, u32[]{:S(2)}) collective-permute-start(f32[768,384]{1,0:T(8,128)} %get-tuple-element.17), channel_id=1, source_target_pairs={{0,1},{1,2},{2,3},{4,5},{5,6},{6,7},{8,9},{9,10},{10,11},{12,13},{... | collective-permute-start | bytes 3538952 | tf_op jit(solution)/shard_map/ppermute | solution.py:218
  86.8 7.0 %collective-permute-done.9.refs_9_ = f32[768,384]{1,0:T(8,128)S(1)} collective-permute-done((f32[768,384]{1,0:T(8,128)S(1)}, f32[768,384]{1,0:T(8,128)S(1)}, u32[]{:S(2)}, u32[]{:S(2)}) %collective-permute-start.9) | collective-permute-done | bytes 1179680 | tf_op jit(solution)/shard_map/ppermute | solution.py:218
  93.9 1.0 copy-done.8
  94.9 1.5 collective-permute-start.6
  97.1 0.8 copy-done.3
  97.9 0.8 copy-done.5
  98.7 0.8 copy-done.7
  99.5 1.9 %shard_map.58 = (f32[25,96,128]{2,1,0:T(8,128)S(1)}, f32[25,96,128]{2,1,0:T(8,128)}) custom-call(f32[96,128]{1,0:T(8,128)S(1)} %copy-done.5, f32[96,128]{1,0:T(8,128)S(1)} %copy-done.7, f32[96,128]{1,0:T(8,128)S(1)} %copy-done.3, f32[96,128]{1,0:T(8,128)S(1)} %copy-done.1), custom_call_target="tpu_custom_call" | custom-call | flops 10000000 | bytes 10000000 | tf_op jit(solution)/shard_map/pallas_call | solution.py:58
  101.4 8.5 %shard_map.59.refs_10_.refs_6_ = bf16[12,2048,256]{2,1,0:T(8,128)(2,1)} custom-call(s32[1]{0:T(128)} %bitcast.5.offset, f32[25,96,128]{2,1,0:T(8,128)S(1)} %get-tuple-element.6.table), custom_call_target="tpu_custom_call" | custom-call | flops 10000000 | bytes 20000000 | tf_op jit(solution)/shard_map/pallas_call | solution.py:98
  110.0 10.4 %shard_map.56.refs_2_.refs_3_ = f32[768,768]{1,0:T(8,128)} custom-call(f32[384,768]{1,0:T(8,128)S(1)} %collective-permute-done.2.refs_0_, f32[1536,3072]{1,0:T(8,128)} %refs_3_.7, f32[1536,3072]{1,0:T(8,128)} %refs_3_.7, f32[1536,3072]{1,0:T(8,128)} %refs_3_.7, f32[1536,3072]{1,0:T(8,128)} %refs_3_.7, f32[384,768]{1,0:T(8,128)} %collective-permute-done.3.refs_5_, ...), custom_call_target="tpu_custom_call" | custom-call | flops 23592960 | bytes 7077888 | tf_op jit(solution)/shard_map/pallas_call | solution.py:161
  120.4 22.8 %shard_map.61.refs_7_ = f32[1536,3072]{1,0:T(8,128)} custom-call(f32[768,384]{1,0:T(8,128)} %collective-permute-done.8.refs_0_, f32[768,3072]{1,0:T(8,128)} %shard_map.60.refs_1_.refs_2_.refs_3_.refs_4_.refs_5_.refs_6_.refs_7_.refs_8_, f32[768,3072]{1,0:T(8,128)} %shard_map.60.refs_1_.refs_2_.refs_3_.refs_4_.refs_5_.refs_6_.refs_7_.refs_8_, ...), custom_call_target="tpu_custom_call" | custom-call | flops 94371840 | bytes 28311552 | tf_op jit(solution)/shard_map/pallas_call | solution.py:201
  143.2 18.1 %shard_map.55.refs_2_.refs_3_.refs_4_.refs_5_.refs_0_.refs_1_ = f32[768,1536]{1,0:T(8,128)} custom-call(f32[384,1536]{1,0:T(8,128)} %collective-permute-done.refs_0_, f32[1536,3072]{1,0:T(8,128)} %refs_3_.7, f32[1536,3072]{1,0:T(8,128)} %refs_3_.7, f32[1536,3072]{1,0:T(8,128)} %refs_3_.7, f32[1536,3072]{1,0:T(8,128)} %refs_3_.7, ...), custom_call_target="tpu_custom_call" | custom-call | flops 47185920 | bytes 14155776 | tf_op jit(solution)/shard_map/pallas_call | solution.py:161
  161.3 12.6 %shard_map.62.refs_7_ = f32[1536,3072]{1,0:T(8,128)} custom-call(f32[768,384]{1,0:T(8,128)S(1)} %collective-permute-done.7.refs_0_, f32[768,768]{1,0:T(8,128)} %shard_map.57.refs_1_.refs_4_, f32[768,1536]{1,0:T(8,128)} %shard_map.55.refs_2_.refs_3_.refs_4_.refs_5_.refs_0_.refs_1_, ...), custom_call_target="tpu_custom_call", output_to_operand_aliasing={{}: (7, {})} | custom-call | flops 47185920 | bytes 14155776 | tf_op jit(solution)/shard_map/pallas_call | solution.py:201
  173.9 12.6 %shard_map.63 = f32[1536,3072]{1,0:T(8,128)} custom-call(f32[768,1536]{1,0:T(8,128)} %shard_map.55.refs_2_.refs_3_.refs_4_.refs_5_.refs_0_.refs_1_, f32[768,1536]{1,0:T(8,128)} %shard_map.55.refs_2_.refs_3_.refs_4_.refs_5_.refs_0_.refs_1_, f32[768,768]{1,0:T(8,128)} %shard_map.56.refs_2_.refs_3_, ...), custom_call_target="tpu_custom_call", output_to_operand_aliasing={{}: (7, {})} | custom-call | flops 47185920 | bytes 14155776 | tf_op jit(solution)/shard_map/pallas_call | solution.py:201
  (29 shorter events, 0.9 us)
Async XLA Ops:
  2.9 55.3 %collective-permute-start.4 = (f32[384,768]{1,0:T(8,128)}, f32[384,768]{1,0:T(8,128)S(1)}, u32[]{:S(2)}, u32[]{:S(2)}) collective-permute-start(f32[384,768]{1,0:T(8,128)} %pad_maximum_fusion), channel_id=1, source_target_pairs={{0,4},{4,8},{8,12},{12,16},{16,20},{20,24},{24,28},{1,5},{5,9},{9,... | collective-permute-start | bytes 3538952 | tf_op jit(solution)/shard_map/ppermute | solution.py:218
  8.5 56.1 %collective-permute-start.5 = (f32[384,768]{1,0:T(8,128)}, f32[384,768]{1,0:T(8,128)}, u32[]{:S(2)}, u32[]{:S(2)}) collective-permute-start(f32[384,768]{1,0:T(8,128)} %pad_maximum_fusion.1), channel_id=1, source_target_pairs={{4,0},{8,4},{12,8},{16,12},{20,16},{24,20},{28,24},{5,1},{9,5},{13... | collective-permute-start | bytes 3538952 | tf_op jit(solution)/shard_map/ppermute | solution.py:218
  13.7 62.7 %collective-permute-start.3 = (f32[384,768]{1,0:T(8,128)}, f32[384,768]{1,0:T(8,128)}, u32[]{:S(2)}, u32[]{:S(2)}) collective-permute-start(f32[384,768]{1,0:T(8,128)} %get-tuple-element.11), channel_id=1, source_target_pairs={{4,0},{8,4},{12,8},{16,12},{20,16},{24,20},{28,24},{5,1},{9,5},{13... | collective-permute-start | bytes 3538952 | tf_op jit(solution)/shard_map/ppermute | solution.py:218
  15.6 10.5 %copy-start = (f32[96,128]{1,0:T(8,128)S(1)}, f32[96,128]{1,0:T(8,128)}, u32[]{:S(2)}) copy-start(f32[96,128]{1,0:T(8,128)} %diffuse_lat.1) | copy-start | bytes 147460
  15.6 10.5 %copy-start.2 = (f32[96,128]{1,0:T(8,128)S(1)}, f32[96,128]{1,0:T(8,128)}, u32[]{:S(2)}) copy-start(f32[96,128]{1,0:T(8,128)} %diffuse_lon.1) | copy-start | bytes 147460
  15.6 10.6 %copy-start.4 = (f32[96,128]{1,0:T(8,128)S(1)}, f32[96,128]{1,0:T(8,128)}, u32[]{:S(2)}) copy-start(f32[96,128]{1,0:T(8,128)} %east_wind.1) | copy-start | bytes 147460
  15.6 10.6 %copy-start.6 = (f32[96,128]{1,0:T(8,128)S(1)}, f32[96,128]{1,0:T(8,128)}, u32[]{:S(2)}) copy-start(f32[96,128]{1,0:T(8,128)} %north_wind.1) | copy-start | bytes 147460
  15.6 69.0 %collective-permute-start.2 = (f32[384,768]{1,0:T(8,128)}, f32[384,768]{1,0:T(8,128)S(1)}, u32[]{:S(2)}, u32[]{:S(2)}) collective-permute-start(f32[384,768]{1,0:T(8,128)} %get-tuple-element.12), channel_id=1, source_target_pairs={{0,4},{4,8},{8,12},{12,16},{16,20},{20,24},{24,28},{1,5},{5,9},{9,... | collective-permute-start | bytes 3538952 | tf_op jit(solution)/shard_map/ppermute | solution.py:218
  24.2 119.0 %collective-permute-start.1 = (f32[384,1536]{1,0:T(8,128)}, f32[384,1536]{1,0:T(8,128)}, u32[]{:S(2)}, u32[]{:S(2)}) collective-permute-start(f32[384,1536]{1,0:T(8,128)} %get-tuple-element.13), channel_id=1, source_target_pairs={{4,0},{8,4},{12,8},{16,12},{20,16},{24,20},{28,24},{5,1},{9,5},{13... | collective-permute-start | bytes 7077896 | tf_op jit(solution)/shard_map/ppermute | solution.py:218
  58.1 85.0 %collective-permute-start = (f32[384,1536]{1,0:T(8,128)}, f32[384,1536]{1,0:T(8,128)}, u32[]{:S(2)}, u32[]{:S(2)}) collective-permute-start(f32[384,1536]{1,0:T(8,128)} %get-tuple-element.14), channel_id=1, source_target_pairs={{0,4},{4,8},{8,12},{12,16},{16,20},{20,24},{24,28},{1,5},{5,9},{9,... | collective-permute-start | bytes 7077896 | tf_op jit(solution)/shard_map/ppermute | solution.py:218
  64.6 29.3 %collective-permute-start.9 = (f32[768,384]{1,0:T(8,128)S(1)}, f32[768,384]{1,0:T(8,128)S(1)}, u32[]{:S(2)}, u32[]{:S(2)}) collective-permute-start(f32[768,384]{1,0:T(8,128)S(1)} %get-tuple-element.15), channel_id=1, source_target_pairs={{1,0},{2,1},{3,2},{5,4},{6,5},{7,6},{9,8},{10,9},{11,10},{13,12},{... | collective-permute-start | bytes 3538952 | tf_op jit(solution)/shard_map/ppermute | solution.py:218
  76.3 44.0 %collective-permute-start.8 = (f32[768,384]{1,0:T(8,128)}, f32[768,384]{1,0:T(8,128)}, u32[]{:S(2)}, u32[]{:S(2)}) collective-permute-start(f32[768,384]{1,0:T(8,128)} %get-tuple-element.16), channel_id=1, source_target_pairs={{0,1},{1,2},{2,3},{4,5},{5,6},{6,7},{8,9},{9,10},{10,11},{12,13},{... | collective-permute-start | bytes 3538952 | tf_op jit(solution)/shard_map/ppermute | solution.py:218
  84.6 76.7 %collective-permute-start.7 = (f32[768,384]{1,0:T(8,128)}, f32[768,384]{1,0:T(8,128)S(1)}, u32[]{:S(2)}, u32[]{:S(2)}) collective-permute-start(f32[768,384]{1,0:T(8,128)} %get-tuple-element.17), channel_id=1, source_target_pairs={{0,1},{1,2},{2,3},{4,5},{5,6},{6,7},{8,9},{9,10},{10,11},{12,13},{... | collective-permute-start | bytes 3538952 | tf_op jit(solution)/shard_map/ppermute | solution.py:218
  93.9 1.0 copy-start.8
  94.9 79.0 %collective-permute-start.6 = (f32[768,384]{1,0:T(8,128)}, f32[768,384]{1,0:T(8,128)S(1)}, u32[]{:S(2)}, u32[]{:S(2)}) collective-permute-start(f32[768,384]{1,0:T(8,128)} %get-tuple-element.18), channel_id=1, source_target_pairs={{1,0},{2,1},{3,2},{5,4},{6,5},{7,6},{9,8},{10,9},{11,10},{13,12},{... | collective-permute-start | bytes 3538952 | tf_op jit(solution)/shard_map/ppermute | solution.py:218
  96.3 0.8 copy-start.1
  97.1 0.8 copy-start.3
  97.9 0.8 copy-start.5
  98.7 0.8 copy-start.7
where the time goes:
time: 189 us; the launch traced here: 186 us
  Pallas kernels  126 us (67%)
  starting transfers between devices  27.6 us (15%)
  local copies, waits for them, and re-layouts  23.1 us (12%)
  waiting for transfers between devices  7.06 us (4%)
  other arithmetic  2.29 us (1%)
    pallas_call x4, Pallas kernels, column_sweep(): pl.pallas_call(functools.partial(column_kernel, arrays, sides), grid=(wid...  67.8 us
    pallas_call x3, Pallas kernels, row_sweep(): pl.pallas_call(functools.partial(row_kernel, count), grid=(rows // BLOCK,...  48 us
    ppermute x10, starting transfers between devices, exchange(): return (lax.ppermute(last, axis, up), lax.ppermute(first, axis, down))  27.6 us
    slice x3, local copies, waits for them, and re-layouts, columns(): covariance[low:high, a * UNIT:b * UNIT]  9.78 us
    pallas_call x1, Pallas kernels, blocks_of(): pl.pallas_call(functools.partial(block_kernel, made, transposed), grid=(g...  8.54 us
    ppermute x10, waiting for transfers between devices, exchange(): return (lax.ppermute(last, axis, up), lax.ppermute(first, axis, down))  7.06 us
    unnamed x18, local copies, waits for them, and re-layouts  4.22 us
  transfers between devices with their start and end apart: 10, of which 1 were waited for; matrix products, arithmetic and copies ran while one was open for 10% of the time, Pallas kernels for 61%

commit v1 on v0

--- a/solution.py
+++ b/solution.py
@@ -319,9 +319,442 @@
     return out
 
 
+LANES = 128
+SUBS = 8
+PAD = 8
+HALO = STEPS * NLON
+PAIR = 2
+RBLOCK = 32
+MESH = pl.DeviceIdType.MESH
+
+
+def tile_order(tiles):
+    edges = list(range(STEPS)) + list(range(tiles - STEPS, tiles))
+    return edges, list(range(STEPS, tiles - STEPS))
+
+
+def detours(row_devices, tiles):
+    if row_devices != 8:
+        return None
+    _, middle = tile_order(tiles)
+    carried = [t for n, t in enumerate(middle) if n % 3]
+    return dict(low=3, high=4, up_by=7, down_by=0, tiles=carried)
+
+
+def fused_kernel(row_devices, col_devices, lines, tiles, cov, ew, nw, dlon, dlat, out, relay, big, fwd, one, two, pads, ctab, rtab,
+                 load_sem, up_send, up_recv, down_send, down_recv, hop_send, hop_recv, z_send, z_recv, out_sem):
+    r, c = lax.axis_index("row"), lax.axis_index("col")
+    rows = lines * NLON
+    edges, middle = tile_order(tiles)
+    detour = detours(row_devices, tiles)
+    carried = detour["tiles"] if detour else []
+    has_up, has_down = r < row_devices - 1, r > 0
+    has_right, has_left = c < col_devices - 1, c > 0
+
+    partners = [(has_up, {"row": jnp.minimum(r + 1, row_devices - 1)}), (has_down, {"row": jnp.maximum(r - 1, 0)})]
+    partners += [(has_right, {"col": jnp.minimum(c + 1, col_devices - 1)}), (has_left, {"col": jnp.maximum(c - 1, 0)})]
+    if detour:
+        for a in (detour["low"], detour["high"]):
+            for b in (detour["up_by"], detour["down_by"]):
+                partners += [(r == a, {"row": b}), (r == b, {"row": a})]
+    barrier = pltpu.get_barrier_semaphore()
+    count = 0
+    for there, place in partners:
+        count = count + there.astype(jnp.int32)
+
+        @pl.when(there)
+        def _():
+            pl.semaphore_signal(barrier, inc=1, device_id=place, device_id_type=MESH)
+
+    def load(t):
+        return pltpu.make_async_copy(cov.at[:, pl.ds(pl.multiple_of(t * LANES, LANES), LANES)], big.at[t, pl.ds(PAD + HALO, rows), :], load_sem.at[t])
+
+    def lanes(t):
+        return pl.ds(pl.multiple_of(t * LANES, LANES), LANES)
+
+    top, bottom = pl.ds(0, HALO), pl.ds(rows - HALO, HALO)
+    before, after = pl.ds(PAD, HALO), pl.ds(PAD + HALO + rows, HALO)
+
+    def up(t):
+        return pltpu.make_async_remote_copy(cov.at[bottom, lanes(t)], big.at[t, before, :], up_send.at[t], up_recv.at[t],
+                                            device_id={"row": jnp.minimum(r + 1, row_devices - 1)}, device_id_type=MESH)
+
+    def down(t):
+        return pltpu.make_async_remote_copy(cov.at[top, lanes(t)], big.at[t, after, :], down_send.at[t], down_recv.at[t],
+                                            device_id={"row": jnp.maximum(r - 1, 0)}, device_id_type=MESH)
+
+    def up_first(k, t):
+        return pltpu.make_async_remote_copy(cov.at[bottom, lanes(t)], relay.at[k], up_send.at[t], hop_recv.at[k],
+                                            device_id={"row": detour["up_by"]}, device_id_type=MESH)
+
+    def down_first(k, t):
+        return pltpu.make_async_remote_copy(cov.at[top, lanes(t)], relay.at[k], down_send.at[t], hop_recv.at[k],
+                                            device_id={"row": detour["down_by"]}, device_id_type=MESH)
+
+    def up_second(k, t):
+        return pltpu.make_async_remote_copy(relay.at[k], big.at[t, before, :], hop_send.at[k], up_recv.at[t],
+                                            device_id={"row": detour["high"]}, device_id_type=MESH)
+
+    def down_second(k, t):
+        return pltpu.make_async_remote_copy(relay.at[k], big.at[t, after, :], hop_send.at[k], down_recv.at[t],
+                                            device_id={"row": detour["low"]}, device_id_type=MESH)
+
+    for t in edges:
+        load(t).start()
+    pl.semaphore_wait(barrier, count)
+
+    for t in edges + middle:
+        if t in carried:
+            k = carried.index(t)
+            low, high = r == detour["low"], r == detour["high"]
+
+            @pl.when(low)
+            def _():
+                up_first(k, t).start()
+
+            @pl.when(high)
+            def _():
+                down_first(k, t).start()
+        else:
+            low = high = r < 0
+
+        @pl.when(has_up & ~low)
+        def _():
+            up(t).start()
+
+        @pl.when(has_down & ~high)
+        def _():
+            down(t).start()
+    for t in middle:
+        load(t).start()
+
+    def relay_step(k):
+        t = carried[k]
+
+        @pl.when(r == detour["up_by"])
+        def _():
+            up_first(k, t).wait_recv()
+            up_second(k, t).start()
+
+        @pl.when(r == detour["down_by"])
+        def _():
+            down_first(k, t).wait_recv()
+            down_second(k, t).start()
+
+    east_wind, north_wind, lon, lat = ew[...], nw[...], dlon[...], dlat[...]
+    half_east, half_north = 0.5 * east_wind, 0.5 * north_wind
+    made = [1.0 - 2.0 * lon - 2.0 * lat, lon - half_east, lon + half_east, lat - half_north, lat + half_north]
+    grid_lines = lon.shape[0]
+    edge = STEPS - 1
+    spread = -(-(lines + 2 * edge) // SUBS) * SUBS
+    for k, table in enumerate(made):
+        pads[k, pl.ds(0, PAD), :] = jnp.zeros((PAD, LANES), jnp.float32)
+        pads[k, pl.ds(PAD, grid_lines), :] = table
+        pads[k, pl.ds(PAD + grid_lines, spread), :] = jnp.zeros((spread, LANES), jnp.float32)
+    wide = -(-(tiles + 2 * edge) // SUBS) * SUBS
+    for k in range(len(made)):
+        rtab[k] = pads[k, pl.ds(c * tiles + PAD - edge, wide), :]
+        mine = pads[k, pl.ds(r * lines + PAD - edge, spread), :]
+        turned = jnp.transpose(jnp.concatenate([mine, jnp.zeros((LANES - spread, LANES), jnp.float32)], axis=0))
+        for i in range(lines + 2 * edge):
+            ctab[k, i] = jnp.broadcast_to(turned[:, i : i + 1], (NLON, LANES))
+
+    @pl.when(~has_down)
+    def _():
+        def clear(t, _):
+            big[t, before, :] = jnp.zeros((HALO, LANES), jnp.float32)
+            return 0
+        lax.fori_loop(0, tiles, clear, 0)
+
+    @pl.when(~has_up)
+    def _():
+        def clear(t, _):
+            big[t, after, :] = jnp.zeros((HALO, LANES), jnp.float32)
+            return 0
+        lax.fori_loop(0, tiles, clear, 0)
+
+    @pl.when(~has_left)
+    def _():
+        fwd[pl.ds(0, STEPS)] = jnp.zeros((STEPS, rows, LANES), jnp.float32)
+
+    @pl.when(~has_right)
+    def _():
+        fwd[pl.ds(tiles + STEPS, STEPS)] = jnp.zeros((STEPS, rows, LANES), jnp.float32)
+
+    sub = lax.broadcasted_iota(jnp.int32, (SUBS, LANES), 0)
+
+    def line_step(line, load_from, store_to):
+        for g in range(NLON // SUBS):
+            at = g * SUBS
+            coef = [ctab[k, line - 1, pl.ds(at, SUBS), :] for k in range(5)]
+            for n in range(PAIR):
+                ref, base = load_from(n)
+                base = pl.multiple_of(base, SUBS)
+                here = ref[pl.ds(base + at, SUBS), :]
+                east = ref[pl.ds(base + at + 1, SUBS), :]
+                west = ref[pl.ds(base + at - 1, SUBS), :]
+                if g == NLON // SUBS - 1:
+                    east = jnp.where(sub == SUBS - 1, ref[pl.ds(base, 1), :], east)
+                if g == 0:
+                    west = jnp.where(sub == 0, ref[pl.ds(base + NLON - 1, 1), :], west)
+                north = ref[pl.ds(base + at + NLON, SUBS), :]
+                south = ref[pl.ds(base + at - NLON, SUBS), :]
+                value = (coef[0] * here + coef[1] * east) + (coef[2] * west + coef[3] * north) + coef[4] * south
+                to, start = store_to(n)
+                to[pl.ds(pl.multiple_of(start + at, SUBS), SUBS), :] = value
+
+    def column_pass(pair, lo, hi):
+        first = lo - 2
+
+        def row(line):
+            return PAD + (line - first) * NLON
+
+        def step1(line, _):
+            line_step(line, lambda n: (big.at[pair[n]], PAD + line * NLON), lambda n: (one.at[n], row(line)))
+            return 0
+
+        def step2(line, _):
+            line_step(line, lambda n: (one.at[n], row(line)), lambda n: (two.at[n], row(line)))
+            return 0
+
+        def step3(line, _):
+            line_step(line, lambda n: (two.at[n], row(line)), lambda n: (fwd.at[pair[n] + STEPS], (line - STEPS) * NLON))
+            return 0
+
+        lax.fori_loop(lo - 2, hi + 2, step1, 0)
+        lax.fori_loop(lo - 1, hi + 1, step2, 0)
+        lax.fori_loop(lo, hi, step3, 0)
+
+    def row_pass(a, b, start, stop, store):
+        def block(i, _):
+            at = pl.multiple_of(start + i * RBLOCK, RBLOCK)
+            got = {}
+            for tile in range(a - STEPS, b + STEPS):
+                got[0, tile] = fwd[tile + STEPS, pl.ds(at, RBLOCK), :]
+                for step in range(1, STEPS + 1):
+                    mid = tile - step
+                    if mid < a - STEPS + step:
+                        continue
+                    here = got[step - 1, mid]
+                    coef = [rtab[k, pl.ds(mid + edge, 1), :] for k in range(5)]
+                    value = (
+                        (coef[0] * here + coef[1] * pltpu.roll(here, LANES - 1, 1))
+                        + (coef[2] * pltpu.roll(here, 1, 1) + coef[3] * got[step - 1, mid + 1])
+                        + coef[4] * got[step - 1, mid - 1]
+                    )
+                    got.pop((step - 1, mid - 1))
+                    if step < STEPS:
+                        got[step, mid] = value
+                    else:
+                        store(mid, at, value)
+            return 0
+
+        lax.fori_loop(0, (stop - start) // RBLOCK, block, 0)
+
+    inner = pl.ds(HALO, rows - 2 * HALO)
+
+    def z_copy(part, right):
+        where = (inner, top, bottom)[part]
+        first, there = (tiles, 0) if right else (STEPS, tiles + STEPS)
+        other = jnp.minimum(c + 1, col_devices - 1) if right else jnp.maximum(c - 1, 0)
+        n = 2 * part + (1 if right else 0)
+        return pltpu.make_async_remote_copy(fwd.at[pl.ds(first, STEPS), where, :], fwd.at[pl.ds(there, STEPS), where, :],
+                                            z_send.at[n], z_recv.at[n], device_id={"col": other}, device_id_type=MESH)
+
+    def z_start(part):
+        @pl.when(has_right)
+        def _():
+            z_copy(part, True).start()
+
+        @pl.when(has_left)
+        def _():
+            z_copy(part, False).start()
+
+    def z_wait(part):
+        @pl.when(has_right)
+        def _():
+            z_copy(part, True).wait_send()
+            z_copy(part, False).wait_recv()
+
+        @pl.when(has_left)
+        def _():
+            z_copy(part, False).wait_send()
+            z_copy(part, True).wait_recv()
+
+    def inner_out(t):
+        return pltpu.make_async_copy(fwd.at[t + STEPS, inner, :], out.at[inner, lanes(t)], out_sem.at[0, t])
+
+    def outer_out(side, t):
+        rows_there = bottom if side else top
+        return pltpu.make_async_copy(big.at[t, pl.ds(PAD + HALO + (rows - HALO if side else 0), HALO), :], out.at[rows_there, lanes(t)], out_sem.at[1 + side, t])
+
+    def arrive(t):
+        @pl.when(has_down)
+        def _():
+            up(t).wait_recv()
+
+        @pl.when(has_up)
+        def _():
+            down(t).wait_recv()
+
+    inner_lines = (2 * STEPS, lines)
+    north_lines, south_lines = (STEPS, 2 * STEPS), (lines, lines + STEPS)
+
+    pairs = [edges[n : n + PAIR] for n in range(0, len(edges), PAIR)]
+    for pair in pairs:
+        for t in pair:
+            load(t).wait()
+        column_pass(pair, *inner_lines)
+    z_start(0)
+
+    steps = len(carried)
+    middle_pairs = len(middle) // PAIR
+    taken = 0
+    group = 3
+    for at in range(0, middle_pairs, group):
+        n = min(group, middle_pairs - at)
+
+        def some(i, _):
+            t = middle[0] + (at + i) * PAIR
+            for m in range(PAIR):
+                load(t + m).wait()
+            column_pass([t + m for m in range(PAIR)], *inner_lines)
+            return 0
+
+        lax.fori_loop(0, n, some, 0)
+        while taken < steps * (at + n) // middle_pairs:
+            relay_step(taken)
+            taken += 1
+
+    for pair in pairs:
+        for t in pair:
+            arrive(t)
+        column_pass(pair, *north_lines)
+        column_pass(pair, *south_lines)
+    z_start(1)
+    z_start(2)
+
+    z_wait(0)
+
+    def keep_inner(tile, at, value):
+        fwd[tile + STEPS, pl.ds(at, RBLOCK), :] = value
+
+    row_pass(0, tiles, HALO, rows - HALO, keep_inner)
+    for t in range(tiles):
+        inner_out(t).start()
+
+    def keep_outer(tile, at, value):
+        big[tile, pl.ds(pl.multiple_of(PAD + HALO + at, SUBS), RBLOCK), :] = value
+
+    done = 0
+    waited = False
+    for at in range(0, middle_pairs, group):
+        n = min(group, middle_pairs - at)
+
+        def some(i, _):
+            t = middle[0] + (at + i) * PAIR
+            for m in range(PAIR):
+                arrive(t + m)
+            pair = [t + m for m in range(PAIR)]
+            column_pass(pair, *north_lines)
+            column_pass(pair, *south_lines)
+            return 0
+
+        lax.fori_loop(0, n, some, 0)
+        last = at + n == middle_pairs
+        upto = tiles if last else middle[0] + (at + n) * PAIR - STEPS
+        if not last and at == 0:
+            continue
+        if not waited:
+            z_wait(1)
+            z_wait(2)
+            waited = True
+        row_pass(done, upto, 0, HALO, keep_outer)
+        row_pass(done, upto, rows - HALO, rows, keep_outer)
+        for t in range(done, upto):
+            outer_out(0, t).start()
+            outer_out(1, t).start()
+        done = upto
+
+    for t in range(tiles):
+        if t in carried:
+            low, high = r == detour["low"], r == detour["high"]
+        else:
+            low = high = r < 0
+        k = carried.index(t) if t in carried else 0
+
+        @pl.when(has_up)
+        def _():
+            up(t).wait_send()
+
+        @pl.when(has_down)
+        def _():
+            down(t).wait_send()
+    for k, t in enumerate(carried):
+        @pl.when(r == detour["up_by"])
+        def _():
+            up_second(k, t).wait_send()
+
+        @pl.when(r == detour["down_by"])
+        def _():
+            down_second(k, t).wait_send()
+    for t in range(tiles):
+        inner_out(t).wait()
+        outer_out(0, t).wait()
+        outer_out(1, t).wait()
+
+
+def fused_body(row_devices, col_devices, covariance, east_wind, north_wind, diffuse_lon, diffuse_lat):
+    rows, cols = covariance.shape
+    lines, tiles = rows // NLON, cols // NLON
+    edge = STEPS - 1
+    spread = -(-(lines + 2 * edge) // SUBS) * SUBS
+    wide = -(-(tiles + 2 * edge) // SUBS) * SUBS
+    slack = PAD + east_wind.shape[0] + max(spread, wide)
+    detour = detours(row_devices, tiles)
+    hops = len(detour["tiles"]) if detour else 1
+    deep = lines - 2 * STEPS + 4
+    f32 = jnp.float32
+    out, _ = pl.pallas_call(
+        functools.partial(fused_kernel, row_devices, col_devices, lines, tiles),
+        in_specs=[pl.BlockSpec(memory_space=pl.ANY)] + [pl.BlockSpec(memory_space=pltpu.VMEM)] * 4,
+        out_specs=[pl.BlockSpec(memory_space=pl.ANY)] * 2,
+        out_shape=[jax.ShapeDtypeStruct((rows, cols), f32), jax.ShapeDtypeStruct((hops, HALO, LANES), f32)],
+        scratch_shapes=[
+            pltpu.VMEM((tiles, 2 * PAD + 2 * HALO + rows, LANES), f32),
+            pltpu.VMEM((tiles + 2 * STEPS, rows, LANES), f32),
+            pltpu.VMEM((PAIR, 2 * PAD + deep * NLON, LANES), f32),
+            pltpu.VMEM((PAIR, 2 * PAD + deep * NLON, LANES), f32),
+            pltpu.VMEM((5, slack, LANES), f32),
+            pltpu.VMEM((5, lines + 2 * edge, NLON, LANES), f32),
+            pltpu.VMEM((5, wide, LANES), f32),
+            pltpu.SemaphoreType.DMA((tiles,)),
+            pltpu.SemaphoreType.DMA((tiles,)),
+            pltpu.SemaphoreType.DMA((tiles,)),
+            pltpu.SemaphoreType.DMA((tiles,)),
+            pltpu.SemaphoreType.DMA((tiles,)),
+            pltpu.SemaphoreType.DMA((hops,)),
+            pltpu.SemaphoreType.DMA((hops,)),
+            pltpu.SemaphoreType.DMA((6,)),
+            pltpu.SemaphoreType.DMA((6,)),
+            pltpu.SemaphoreType.DMA((3, tiles)),
+        ],
+        compiler_params=pltpu.CompilerParams(collective_id=0, has_side_effects=True, vmem_limit_bytes=64 * 1024 * 1024),
+    )(covariance, east_wind, north_wind, diffuse_lon, diffuse_lat)
+    return out
+
+
 def solution(mesh):
+    row_devices, col_devices = mesh.shape["row"], mesh.shape["col"]
+
+    def run(covariance, *tables):
+        lines, tiles = covariance.shape[0] // NLON, covariance.shape[1] // NLON
+        if lines > 2 * STEPS and tiles >= 4 * STEPS and (tiles - 2 * STEPS) % PAIR == 0:
+            return fused_body(row_devices, col_devices, covariance, *tables)
+        return body(covariance, *tables)
+
     return jax.shard_map(
-        body,
+        run,
         mesh=mesh,
         in_specs=(P("row", "col"), P(), P(), P(), P()),
         out_specs=P("row", "col"),

time: 189 us -> 143 us (0.76)
  starting transfers between devices: 27.6 us -> 0 us
  local copies, waits for them, and re-layouts: 23.1 us -> 14.8 us
  waiting for transfers between devices: 7.06 us -> 0 us
  other arithmetic: 2.29 us -> 0 us
    ppermute x10 -> x0, starting transfers between devices: 27.6 us -> none  [exchange(): return (lax.ppermute(last, axis, up), lax.ppermute(first, axis, down))]
    slice x5 -> x0, local copies, waits for them, and re-layouts: 15.8 us -> none  [the longest x3 9.78 us: columns(): covariance[low:high, a * UNIT:b * UNIT]]
    unnamed x18 -> x1, local copies, waits for them, and re-layouts: 4.22 us -> 14.8 us
    ppermute x10 -> x0, waiting for transfers between devices: 7.06 us -> none  [exchange(): return (lax.ppermute(last, axis, up), lax.ppermute(first, axis, down))]
    broadcast_in_dim x1 -> x0, local copies, waits for them, and re-layouts: 3.09 us -> none  [body(): jnp.broadcast_to(row_coefs[:, :, :, None], row_coefs.shape + (NLON,))]
    concatenate x2 -> x0, other arithmetic: 2.24 us -> none  [columns(): jnp.concatenate([covariance[low:high, a * UNIT:b * UNIT] for a, b in part...]
    pallas_call x9 -> x1, Pallas kernels: 126 us -> 126 us  [fused_body(): pl.pallas_call(functools.partial(fused_kernel, row_devices, col_devices,...]
  transfers between devices with their start and end apart: 10 -> 0, of which waited for: 1 -> 0; matrix products, arithmetic and copies ran while one was open for 10% -> 0% of each run, Pallas kernels for 61% -> 0%
where the time goes in v1:
time: 143 us; the launch traced here: 141 us
  Pallas kernels  126 us (88%)
  local copies, waits for them, and re-layouts  14.8 us (10%)
    pallas_call x1, Pallas kernels, fused_body(): pl.pallas_call(functools.partial(fused_kernel, row_devices, col_devices,...  126 us
    unnamed x1, local copies, waits for them, and re-layouts  14.8 us

profile of v1, /device:TPU:1, one launch (start us, length us, event | category | flops | bytes accessed | tf_op | source)
XLA Modules:
  0.0 140.9 jit_solution(6987234893705671708)
XLA Ops:
  0.0 126.1 %shard_map.55 = (f32[1536,3072]{1,0:T(8,128)}, f32[12,384,128]{2,1,0:T(8,128)}) custom-call(f32[1536,3072]{1,0:T(8,128)} %cov.1, f32[96,128]{1,0:T(8,128)} %ew.1, f32[96,128]{1,0:T(8,128)} %nw.1, f32[96,128]{1,0:T(8,128)} %dlon.1, f32[96,128]{1,0:T(8,128)} %dlat.1), custom_call_target="tpu_custom_call" | custom-call | tf_op jit(solution)/shard_map/pallas_call | solution.py:718
  126.1 14.8 %copy.7 = f32[1536,3072]{1,0:T(8,128)} copy(f32[1536,3072]{1,0:T(8,128)} %get-tuple-element.6) | data formatting | bytes 37748736

commit v2 on v1

--- a/solution.py
+++ b/solution.py
@@ -324,7 +324,8 @@
 PAD = 8
 HALO = STEPS * NLON
 PAIR = 2
-RBLOCK = 32
+RBLOCK = 96
+PIECE = 192
 MESH = pl.DeviceIdType.MESH
 
 
@@ -341,8 +342,8 @@
     return dict(low=3, high=4, up_by=7, down_by=0, tiles=carried)
 
 
-def fused_kernel(row_devices, col_devices, lines, tiles, cov, ew, nw, dlon, dlat, out, relay, big, fwd, one, two, pads, ctab, rtab,
-                 load_sem, up_send, up_recv, down_send, down_recv, hop_send, hop_recv, z_send, z_recv, out_sem):
+def fused_kernel(row_devices, col_devices, lines, tiles, cov, ew, nw, dlon, dlat, fwd, rtab, relay, big, one, two, pads, ctab,
+                 load_sem, up_send, up_recv, down_send, down_recv, hop_send, hop_recv, z_send, z_recv):
     r, c = lax.axis_index("row"), lax.axis_index("col")
     rows = lines * NLON
     edges, middle = tile_order(tiles)
@@ -483,85 +484,151 @@
 
     sub = lax.broadcasted_iota(jnp.int32, (SUBS, LANES), 0)
 
-    def line_step(line, load_from, store_to):
+    def line_step(pair, line, source, stores, keeps=()):
         for g in range(NLON // SUBS):
             at = g * SUBS
             coef = [ctab[k, line - 1, pl.ds(at, SUBS), :] for k in range(5)]
-            for n in range(PAIR):
-                ref, base = load_from(n)
-                base = pl.multiple_of(base, SUBS)
-                here = ref[pl.ds(base + at, SUBS), :]
-                east = ref[pl.ds(base + at + 1, SUBS), :]
-                west = ref[pl.ds(base + at - 1, SUBS), :]
+            for n in range(len(pair)):
+
+                def read(d, shift=0, count=SUBS):
+                    ref, base = source(n, d)
+                    return ref[pl.ds(pl.multiple_of(base, SUBS) + shift, count), :]
+
+                def write(place, value):
+                    ref, base = place
+                    ref[pl.ds(pl.multiple_of(base + at, SUBS), SUBS), :] = value
+
+                seen = {d: read(d, at) for d in (-1, 0, 1)}
+                east, west = read(0, at + 1), read(0, at - 1)
                 if g == NLON // SUBS - 1:
-                    east = jnp.where(sub == SUBS - 1, ref[pl.ds(base, 1), :], east)
+                    east = jnp.where(sub == SUBS - 1, read(0, 0, 1), east)
                 if g == 0:
-                    west = jnp.where(sub == 0, ref[pl.ds(base + NLON - 1, 1), :], west)
-                north = ref[pl.ds(base + at + NLON, SUBS), :]
-                south = ref[pl.ds(base + at - NLON, SUBS), :]
-                value = (coef[0] * here + coef[1] * east) + (coef[2] * west + coef[3] * north) + coef[4] * south
-                to, start = store_to(n)
-                to[pl.ds(pl.multiple_of(start + at, SUBS), SUBS), :] = value
-
-    def column_pass(pair, lo, hi):
-        first = lo - 2
-
-        def row(line):
-            return PAD + (line - first) * NLON
+                    west = jnp.where(sub == 0, read(0, NLON - 1, 1), west)
+                value = (coef[0] * seen[0] + coef[1] * east) + (coef[2] * west + coef[3] * seen[1]) + coef[4] * seen[-1]
+                for place in stores(n):
+                    write(place, value)
+                for d, place in keeps:
+                    write(place(n), seen[d])
+
+    def in_big(pair, n, slot):
+        return big.at[pair[n]], PAD + slot * NLON
+
+    def in_fwd(pair, n, line):
+        return fwd.at[pair[n] + STEPS], (line - STEPS) * NLON
+
+    def inner_columns(pair):
+        kept_one = {4: 5, 5: 6, lines: lines - 1, lines + 1: lines}
+        kept_two = {5: 7, 6: 8, lines - 1: lines - 3, lines: lines - 2}
+
+        def at_one(n, line):
+            return one.at[n], PAD + (line - 4) * NLON
+
+        def at_two(n, line):
+            return two.at[n], PAD + (line - 5) * NLON
 
         def step1(line, _):
-            line_step(line, lambda n: (big.at[pair[n]], PAD + line * NLON), lambda n: (one.at[n], row(line)))
+            line_step(pair, line, lambda n, d: in_big(pair, n, line + d), lambda n: [at_one(n, line)])
             return 0
 
-        def step2(line, _):
-            line_step(line, lambda n: (one.at[n], row(line)), lambda n: (two.at[n], row(line)))
+        def step2(line, keep):
+            places = lambda n: [at_two(n, line)] + ([in_big(pair, n, kept_two[line])] if keep else [])
+            keeps = [(d, functools.partial(lambda n, slot: in_big(pair, n, slot), slot=kept_one[line + d]))
+                     for d in ((-1, 0) if line == 5 else (0, 1))] if keep and line in (5, lines) else []
+            line_step(pair, line, lambda n, d: at_one(n, line + d), places, keeps)
+
+        def step2_plain(line, _):
+            step2(line, False)
             return 0
 
         def step3(line, _):
-            line_step(line, lambda n: (two.at[n], row(line)), lambda n: (fwd.at[pair[n] + STEPS], (line - STEPS) * NLON))
+            line_step(pair, line, lambda n, d: at_two(n, line + d), lambda n: [in_fwd(pair, n, line)])
             return 0
 
-        lax.fori_loop(lo - 2, hi + 2, step1, 0)
-        lax.fori_loop(lo - 1, hi + 1, step2, 0)
-        lax.fori_loop(lo, hi, step3, 0)
-
-    def row_pass(a, b, start, stop, store):
-        def block(i, _):
-            at = pl.multiple_of(start + i * RBLOCK, RBLOCK)
-            got = {}
-            for tile in range(a - STEPS, b + STEPS):
-                got[0, tile] = fwd[tile + STEPS, pl.ds(at, RBLOCK), :]
-                for step in range(1, STEPS + 1):
-                    mid = tile - step
-                    if mid < a - STEPS + step:
-                        continue
-                    here = got[step - 1, mid]
-                    coef = [rtab[k, pl.ds(mid + edge, 1), :] for k in range(5)]
-                    value = (
-                        (coef[0] * here + coef[1] * pltpu.roll(here, LANES - 1, 1))
-                        + (coef[2] * pltpu.roll(here, 1, 1) + coef[3] * got[step - 1, mid + 1])
-                        + coef[4] * got[step - 1, mid - 1]
-                    )
-                    got.pop((step - 1, mid - 1))
-                    if step < STEPS:
-                        got[step, mid] = value
-                    else:
-                        store(mid, at, value)
-            return 0
-
-        lax.fori_loop(0, (stop - start) // RBLOCK, block, 0)
-
-    inner = pl.ds(HALO, rows - 2 * HALO)
+        lax.fori_loop(4, lines + 2, step1, 0)
+        step2(5, True)
+        step2(6, True)
+        lax.fori_loop(7, lines - 1, step2_plain, 0)
+        step2(lines - 1, True)
+        step2(lines, True)
+        lax.fori_loop(6, lines, step3, 0)
+
+    def outer_columns(pair, south):
+        ones = [("one", k) for k in range(STEPS)]
+        twos = [("two", k) for k in range(STEPS)]
+        if south:
+            first = [lines + 2, lines + 1, lines]
+            after_one = [("big", lines - 1), ("big", lines)] + ones
+            after_two = [("big", lines - 3), ("big", lines - 2)] + twos
+        else:
+            first = [1, 2, 3]
+            after_one = ones + [("big", 5), ("big", 6)]
+            after_two = twos + [("big", 7), ("big", 8)]
+
+        def place(n, where):
+            name, k = where
+            if name == "big":
+                return in_big(pair, n, k)
+            return (one if name == "one" else two).at[n], PAD + k * NLON
+
+        for k in range(STEPS):
+            line = first[0] + k
+            line_step(pair, line, lambda n, d: in_big(pair, n, line + d), lambda n: [place(n, ones[k])])
+        for k in range(STEPS):
+            line_step(pair, first[1] + k, lambda n, d: place(n, after_one[k + 1 + d]), lambda n: [place(n, twos[k])])
+        for k in range(STEPS):
+            line = first[2] + k
+            line_step(pair, line, lambda n, d: place(n, after_two[k + 1 + d]), lambda n: [in_fwd(pair, n, line)])
+
+    odd = r % 2 == 1
+    quick, slow = odd_rows(odd, rows)
+
+    def quick_columns(pair):
+        @pl.when(odd)
+        def _():
+            for t in pair:
+                up(t).wait_recv()
+            outer_columns(pair, False)
+
+        @pl.when(~odd)
+        def _():
+            for t in pair:
+                down(t).wait_recv()
+            outer_columns(pair, True)
+
+    def slow_columns(pair):
+        @pl.when(odd)
+        def _():
+            @pl.when(has_up)
+            def _():
+                for t in pair:
+                    down(t).wait_recv()
+            outer_columns(pair, True)
+
+        @pl.when(~odd)
+        def _():
+            @pl.when(has_down)
+            def _():
+                for t in pair:
+                    up(t).wait_recv()
+            outer_columns(pair, False)
+
+    pieces = (rows - 2 * HALO) // PIECE
+    side = HALO // PIECE
+
+    def piece_start(part):
+        on_quick, on_slow = quick + (part - pieces) * PIECE, slow + (part - pieces - side) * PIECE
+        start = jnp.where(part < pieces, HALO + part * PIECE, jnp.where(part < pieces + side, on_quick, on_slow))
+        return pl.multiple_of(start, PIECE)
 
     def z_copy(part, right):
-        where = (inner, top, bottom)[part]
+        where = pl.ds(piece_start(part), PIECE)
         first, there = (tiles, 0) if right else (STEPS, tiles + STEPS)
         other = jnp.minimum(c + 1, col_devices - 1) if right else jnp.maximum(c - 1, 0)
         n = 2 * part + (1 if right else 0)
         return pltpu.make_async_remote_copy(fwd.at[pl.ds(first, STEPS), where, :], fwd.at[pl.ds(there, STEPS), where, :],
                                             z_send.at[n], z_recv.at[n], device_id={"col": other}, device_id_type=MESH)
 
-    def z_start(part):
+    def z_start(part, _):
         @pl.when(has_right)
         def _():
             z_copy(part, True).start()
@@ -569,8 +636,9 @@
         @pl.when(has_left)
         def _():
             z_copy(part, False).start()
-
-    def z_wait(part):
+        return 0
+
+    def z_wait(part, _):
         @pl.when(has_right)
         def _():
             z_copy(part, True).wait_send()
@@ -580,109 +648,75 @@
         def _():
             z_copy(part, False).wait_send()
             z_copy(part, True).wait_recv()
-
-    def inner_out(t):
-        return pltpu.make_async_copy(fwd.at[t + STEPS, inner, :], out.at[inner, lanes(t)], out_sem.at[0, t])
-
-    def outer_out(side, t):
-        rows_there = bottom if side else top
-        return pltpu.make_async_copy(big.at[t, pl.ds(PAD + HALO + (rows - HALO if side else 0), HALO), :], out.at[rows_there, lanes(t)], out_sem.at[1 + side, t])
-
-    def arrive(t):
-        @pl.when(has_down)
-        def _():
-            up(t).wait_recv()
-
-        @pl.when(has_up)
-        def _():
-            down(t).wait_recv()
-
-    inner_lines = (2 * STEPS, lines)
-    north_lines, south_lines = (STEPS, 2 * STEPS), (lines, lines + STEPS)
-
-    pairs = [edges[n : n + PAIR] for n in range(0, len(edges), PAIR)]
-    for pair in pairs:
+        return 0
+
+    def pair_of(i):
+        got = []
+        for n in range(PAIR):
+            m = i * PAIR + n
+            got.append(jnp.where(m < 2 * STEPS, m + (m // STEPS) * (tiles - 2 * STEPS), m - STEPS))
+        return got
+
+    edge_pairs, all_pairs = 2 * STEPS // PAIR, tiles // PAIR
+
+    def early(i, _):
+        pair = pair_of(i)
         for t in pair:
             load(t).wait()
-        column_pass(pair, *inner_lines)
-    z_start(0)
-
-    steps = len(carried)
-    middle_pairs = len(middle) // PAIR
-    taken = 0
-    group = 3
-    for at in range(0, middle_pairs, group):
-        n = min(group, middle_pairs - at)
-
-        def some(i, _):
-            t = middle[0] + (at + i) * PAIR
-            for m in range(PAIR):
-                load(t + m).wait()
-            column_pass([t + m for m in range(PAIR)], *inner_lines)
-            return 0
-
-        lax.fori_loop(0, n, some, 0)
-        while taken < steps * (at + n) // middle_pairs:
-            relay_step(taken)
-            taken += 1
-
-    for pair in pairs:
-        for t in pair:
-            arrive(t)
-        column_pass(pair, *north_lines)
-        column_pass(pair, *south_lines)
-    z_start(1)
-    z_start(2)
-
-    z_wait(0)
-
-    def keep_inner(tile, at, value):
-        fwd[tile + STEPS, pl.ds(at, RBLOCK), :] = value
-
-    row_pass(0, tiles, HALO, rows - HALO, keep_inner)
-    for t in range(tiles):
-        inner_out(t).start()
-
-    def keep_outer(tile, at, value):
-        big[tile, pl.ds(pl.multiple_of(PAD + HALO + at, SUBS), RBLOCK), :] = value
-
-    done = 0
-    waited = False
-    for at in range(0, middle_pairs, group):
-        n = min(group, middle_pairs - at)
-
-        def some(i, _):
-            t = middle[0] + (at + i) * PAIR
-            for m in range(PAIR):
-                arrive(t + m)
-            pair = [t + m for m in range(PAIR)]
-            column_pass(pair, *north_lines)
-            column_pass(pair, *south_lines)
-            return 0
-
-        lax.fori_loop(0, n, some, 0)
-        last = at + n == middle_pairs
-        upto = tiles if last else middle[0] + (at + n) * PAIR - STEPS
-        if not last and at == 0:
-            continue
-        if not waited:
-            z_wait(1)
-            z_wait(2)
-            waited = True
-        row_pass(done, upto, 0, HALO, keep_outer)
-        row_pass(done, upto, rows - HALO, rows, keep_outer)
-        for t in range(done, upto):
-            outer_out(0, t).start()
-            outer_out(1, t).start()
-        done = upto
-
-    for t in range(tiles):
-        if t in carried:
-            low, high = r == detour["low"], r == detour["high"]
-        else:
-            low = high = r < 0
-        k = carried.index(t) if t in carried else 0
-
+        inner_columns(pair)
+        quick_columns(pair)
+
+        @pl.when(i == edge_pairs - 1)
+        def _():
+            lax.fori_loop(0, pieces + side, z_start, 0)
+
+        if detour:
+            for k in range(len(carried)):
+                @pl.when(i == k * all_pairs // len(carried))
+                def _():
+                    relay_step(k)
+        return 0
+
+    lax.fori_loop(0, all_pairs, early, 0)
+
+    def keep(tile, at, value):
+        fwd[tile, pl.ds(at, RBLOCK), :] = value
+
+    def ready_rows(part, _):
+        z_wait(part, 0)
+        row_pass(fwd, rtab, 0, tiles, piece_start(part), PIECE, keep)
+        return 0
+
+    groups = slow_groups(all_pairs - edge_pairs)
+    stops = []
+    at = edge_pairs
+    for n in groups[:-1]:
+        at += n
+        stops.append(at)
+
+    def late(i, _):
+        slow_columns(pair_of(i))
+
+        @pl.when(i == edge_pairs - 1)
+        def _():
+            lax.fori_loop(pieces + side, pieces + 2 * side, z_start, 0)
+            lax.fori_loop(0, pieces + side, ready_rows, 0)
+
+        done = 0
+        for n, stop in enumerate(stops):
+            upto = stop * PAIR - 2 * STEPS
+
+            @pl.when(i == stop - 1)
+            def _():
+                if n == 0:
+                    lax.fori_loop(pieces + side, pieces + 2 * side, z_wait, 0)
+                row_pass(fwd, rtab, done, upto, slow, HALO, keep)
+            done = upto
+        return 0
+
+    lax.fori_loop(0, all_pairs, late, 0)
+
+    def sent(t, _):
         @pl.when(has_up)
         def _():
             up(t).wait_send()
@@ -690,6 +724,9 @@
         @pl.when(has_down)
         def _():
             down(t).wait_send()
+        return 0
+
+    lax.fori_loop(0, tiles, sent, 0)
     for k, t in enumerate(carried):
         @pl.when(r == detour["up_by"])
         def _():
@@ -698,10 +735,78 @@
         @pl.when(r == detour["down_by"])
         def _():
             down_second(k, t).wait_send()
-    for t in range(tiles):
-        inner_out(t).wait()
-        outer_out(0, t).wait()
-        outer_out(1, t).wait()
+
+
+def slow_groups(pairs):
+    groups = []
+    while pairs > 3:
+        groups.append(3)
+        pairs -= 3
+    return groups + [pairs - 1, 1] if pairs > 1 else groups + [pairs]
+
+
+def rest(tiles):
+    pairs = (tiles - 2 * STEPS) // PAIR
+    return STEPS + (pairs - slow_groups(pairs)[-1]) * PAIR - STEPS
+
+
+def odd_rows(odd, rows):
+    return jnp.where(odd, 0, rows - HALO), jnp.where(odd, rows - HALO, 0)
+
+
+def row_pass(fwd, rtab, a, b, start, count, store):
+    edge = STEPS - 1
+
+    def block(i, _):
+        at = pl.multiple_of(start + i * RBLOCK, RBLOCK)
+        got = {}
+        for tile in range(a - STEPS, b + STEPS):
+            got[0, tile] = fwd[tile + STEPS, pl.ds(at, RBLOCK), :]
+            for step in range(1, STEPS + 1):
+                mid = tile - step
+                if mid < a - STEPS + step:
+                    continue
+                here = got[step - 1, mid]
+                coef = [rtab[k, pl.ds(mid + edge, 1), :] for k in range(5)]
+                value = (
+                    (coef[0] * here + coef[1] * pltpu.roll(here, LANES - 1, 1))
+                    + (coef[2] * pltpu.roll(here, 1, 1) + coef[3] * got[step - 1, mid + 1])
+                    + coef[4] * got[step - 1, mid - 1]
+                )
+                got.pop((step - 1, mid - 1))
+                if step < STEPS:
+                    got[step, mid] = value
+                else:
+                    store(mid, at, value)
+        return 0
+
+    lax.fori_loop(0, count // RBLOCK, block, 0)
+
+
+def finish_kernel(tiles, fwd, rtab, out, last, done_sem, slow_sem):
+    rows = out.shape[0]
+    begin = rest(tiles)
+    quick, slow = odd_rows(lax.axis_index("row") % 2 == 1, rows)
+    ready = pl.ds(pl.multiple_of(jnp.where(quick == 0, 0, HALO), SUBS), rows - HALO)
+    late = pl.ds(pl.multiple_of(slow, SUBS), HALO)
+
+    def lanes(t):
+        return pl.ds(t * LANES, LANES)
+
+    copies = [pltpu.make_async_copy(fwd.at[t, ready, :], out.at[ready, lanes(t)], done_sem.at[t]) for t in range(tiles)]
+    copies += [pltpu.make_async_copy(fwd.at[t, late, :], out.at[late, lanes(t)], slow_sem.at[t]) for t in range(begin)]
+    for copy in copies:
+        copy.start()
+
+    def keep(tile, at, value):
+        last[tile - begin, pl.ds(pl.multiple_of(at - slow, SUBS), RBLOCK), :] = value
+
+    row_pass(fwd, rtab, begin, tiles, slow, HALO, keep)
+    ends = [pltpu.make_async_copy(last.at[t - begin], out.at[late, lanes(t)], slow_sem.at[t]) for t in range(begin, tiles)]
+    for copy in ends:
+        copy.start()
+    for copy in copies + ends:
+        copy.wait()
 
 
 def fused_body(row_devices, col_devices, covariance, east_wind, north_wind, diffuse_lon, diffuse_lat):
@@ -713,21 +818,20 @@
     slack = PAD + east_wind.shape[0] + max(spread, wide)
     detour = detours(row_devices, tiles)
     hops = len(detour["tiles"]) if detour else 1
-    deep = lines - 2 * STEPS + 4
     f32 = jnp.float32
-    out, _ = pl.pallas_call(
+    held = (tiles + 2 * STEPS, rows, LANES)
+    room = 64 * 1024 * 1024 - 4 * held[0] * held[1] * held[2] - 1024 * 1024
+    fwd, rtab, _ = pl.pallas_call(
         functools.partial(fused_kernel, row_devices, col_devices, lines, tiles),
         in_specs=[pl.BlockSpec(memory_space=pl.ANY)] + [pl.BlockSpec(memory_space=pltpu.VMEM)] * 4,
-        out_specs=[pl.BlockSpec(memory_space=pl.ANY)] * 2,
-        out_shape=[jax.ShapeDtypeStruct((rows, cols), f32), jax.ShapeDtypeStruct((hops, HALO, LANES), f32)],
+        out_specs=[pl.BlockSpec(memory_space=pltpu.VMEM)] * 2 + [pl.BlockSpec(memory_space=pl.ANY)],
+        out_shape=[pltpu.VMEM(held, f32), jax.ShapeDtypeStruct((5, wide, LANES), f32), jax.ShapeDtypeStruct((hops, HALO, LANES), f32)],
         scratch_shapes=[
             pltpu.VMEM((tiles, 2 * PAD + 2 * HALO + rows, LANES), f32),
-            pltpu.VMEM((tiles + 2 * STEPS, rows, LANES), f32),
-            pltpu.VMEM((PAIR, 2 * PAD + deep * NLON, LANES), f32),
-            pltpu.VMEM((PAIR, 2 * PAD + deep * NLON, LANES), f32),
+            pltpu.VMEM((PAIR, 2 * PAD + (lines - 2) * NLON, LANES), f32),
+            pltpu.VMEM((PAIR, 2 * PAD + (lines - 4) * NLON, LANES), f32),
             pltpu.VMEM((5, slack, LANES), f32),
             pltpu.VMEM((5, lines + 2 * edge, NLON, LANES), f32),
-            pltpu.VMEM((5, wide, LANES), f32),
             pltpu.SemaphoreType.DMA((tiles,)),
             pltpu.SemaphoreType.DMA((tiles,)),
             pltpu.SemaphoreType.DMA((tiles,)),
@@ -735,13 +839,23 @@
             pltpu.SemaphoreType.DMA((tiles,)),
             pltpu.SemaphoreType.DMA((hops,)),
             pltpu.SemaphoreType.DMA((hops,)),
-            pltpu.SemaphoreType.DMA((6,)),
-            pltpu.SemaphoreType.DMA((6,)),
-            pltpu.SemaphoreType.DMA((3, tiles)),
+            pltpu.SemaphoreType.DMA((2 * rows // PIECE,)),
+            pltpu.SemaphoreType.DMA((2 * rows // PIECE,)),
         ],
-        compiler_params=pltpu.CompilerParams(collective_id=0, has_side_effects=True, vmem_limit_bytes=64 * 1024 * 1024),
+        compiler_params=pltpu.CompilerParams(collective_id=0, has_side_effects=True, vmem_limit_bytes=room),
     )(covariance, east_wind, north_wind, diffuse_lon, diffuse_lat)
-    return out
+    return pl.pallas_call(
+        functools.partial(finish_kernel, tiles),
+        in_specs=[pl.BlockSpec(memory_space=pltpu.VMEM)] * 2,
+        out_specs=pl.BlockSpec(memory_space=pl.ANY),
+        out_shape=jax.ShapeDtypeStruct((rows, cols), f32),
+        scratch_shapes=[
+            pltpu.VMEM((tiles - rest(tiles), HALO, LANES), f32),
+            pltpu.SemaphoreType.DMA((tiles,)),
+            pltpu.SemaphoreType.DMA((tiles,)),
+        ],
+        compiler_params=pltpu.CompilerParams(vmem_limit_bytes=room),
+    )(pltpu.with_memory_space_constraint(fwd, pltpu.VMEM), rtab)
 
 
 def solution(mesh):
@@ -749,7 +863,7 @@
 
     def run(covariance, *tables):
         lines, tiles = covariance.shape[0] // NLON, covariance.shape[1] // NLON
-        if lines > 2 * STEPS and tiles >= 4 * STEPS and (tiles - 2 * STEPS) % PAIR == 0:
+        if lines >= 4 * STEPS and tiles >= 4 * STEPS and (tiles - 2 * STEPS) % PAIR == 0:
             return fused_body(row_devices, col_devices, covariance, *tables)
         return body(covariance, *tables)
 

time: 143 us -> 92.6 us (0.65); the launches traced: 141 us -> 92.4 us
  Pallas kernels: 126 us -> 92.4 us
  local copies, waits for them, and re-layouts: 14.8 us -> 0 us
    pallas_call x1, Pallas kernels: 126 us -> 84.7 us  [fused_body(): pl.pallas_call(functools.partial(fused_kernel, row_devices, col_devices,...]
    unnamed x1 -> x0, local copies, waits for them, and re-layouts: 14.8 us -> none
    pallas_call x0 -> x1, Pallas kernels: none -> 7.74 us  [fused_body(): pl.pallas_call(functools.partial(finish_kernel, tiles), in_specs=[pl.Bloc...]
where the time goes in v2:
time: 92.6 us; the launch traced here: 92.4 us
  Pallas kernels  92.4 us (100%)
    pallas_call x1, Pallas kernels, fused_body(): pl.pallas_call(functools.partial(fused_kernel, row_devices, col_devices,...  84.7 us
    pallas_call x1, Pallas kernels, fused_body(): pl.pallas_call(functools.partial(finish_kernel, tiles), in_specs=[pl.Bloc...  7.74 us

profile of v2, /device:TPU:1, one launch (start us, length us, event | category | flops | bytes accessed | tf_op | source)
XLA Modules:
  0.0 92.4 jit_solution(11167249658597434985)
XLA Ops:
  0.0 84.7 %shard_map.55 = (f32[30,1536,128]{2,1,0:T(8,128)S(1)}, f32[5,32,128]{2,1,0:T(8,128)}, f32[12,384,128]{2,1,0:T(8,128)}) custom-call(f32[1536,3072]{1,0:T(8,128)} %cov.1, f32[96,128]{1,0:T(8,128)} %ew.1, f32[96,128]{1,0:T(8,128)} %nw.1, f32[96,128]{1,0:T(8,128)} %dlon.1, f32[96,128]{1,0:T(8,128)} %dlat.1), custom_call_target="tpu_custom_call" | custom-call | tf_op jit(solution)/shard_map/pallas_call | solution.py:824
  84.7 7.7 %shard_map.56 = f32[1536,3072]{1,0:T(8,128)} custom-call(f32[30,1536,128]{2,1,0:T(8,128)S(1)} %get-tuple-element.7.fwd, f32[5,32,128]{2,1,0:T(8,128)} %get-tuple-element.8.rtab), custom_call_target="tpu_custom_call" | custom-call | tf_op jit(solution)/shard_map/pallas_call | solution.py:847

commit v3 on v2

--- a/solution.py
+++ b/solution.py
@@ -1,4 +1,5 @@
 import functools
+import math
 
 import jax
 import jax.numpy as jnp
@@ -342,8 +343,68 @@
     return dict(low=3, high=4, up_by=7, down_by=0, tiles=carried)
 
 
-def fused_kernel(row_devices, col_devices, lines, tiles, cov, ew, nw, dlon, dlat, fwd, rtab, relay, big, one, two, pads, ctab,
-                 load_sem, up_send, up_recv, down_send, down_recv, hop_send, hop_recv, z_send, z_recv):
+def line_step(ctab, pair, line, source, stores, keeps=()):
+    sub = lax.broadcasted_iota(jnp.int32, (SUBS, LANES), 0)
+    for g in range(NLON // SUBS):
+        at = g * SUBS
+        coef = [ctab[k, line - 1, pl.ds(at, SUBS), :] for k in range(5)]
+        for n in range(len(pair)):
+
+            def read(d, shift=0, count=SUBS):
+                ref, base = source(n, d)
+                return ref[pl.ds(pl.multiple_of(base, SUBS) + shift, count), :]
+
+            def write(place, value):
+                ref, base = place
+                ref[pl.ds(pl.multiple_of(base + at, SUBS), SUBS), :] = value
+
+            seen = {d: read(d, at) for d in (-1, 0, 1)}
+            east, west = read(0, at + 1), read(0, at - 1)
+            if g == NLON // SUBS - 1:
+                east = jnp.where(sub == SUBS - 1, read(0, 0, 1), east)
+            if g == 0:
+                west = jnp.where(sub == 0, read(0, NLON - 1, 1), west)
+            value = (coef[0] * seen[0] + coef[1] * east) + (coef[2] * west + coef[3] * seen[1]) + coef[4] * seen[-1]
+            for place in stores(n):
+                write(place, value)
+            for d, place in keeps:
+                write(place(n), seen[d])
+
+
+def line_of(big, pair, n, slot):
+    return big.at[pair[n]], PAD + slot * NLON
+
+
+def outer_columns(big, ctab, one, two, lines, pair, south, result):
+    ones = [("one", k) for k in range(STEPS)]
+    twos = [("two", k) for k in range(STEPS)]
+    if south:
+        first = [lines + 2, lines + 1, lines]
+        after_one = [("big", lines - 1), ("big", lines)] + ones
+        after_two = [("big", lines - 3), ("big", lines - 2)] + twos
+    else:
+        first = [1, 2, 3]
+        after_one = ones + [("big", 5), ("big", 6)]
+        after_two = twos + [("big", 7), ("big", 8)]
+
+    def place(n, where):
+        name, k = where
+        if name == "big":
+            return line_of(big, pair, n, k)
+        return (one if name == "one" else two).at[n], PAD + k * NLON
+
+    for k in range(STEPS):
+        line = first[0] + k
+        line_step(ctab, pair, line, lambda n, d: line_of(big, pair, n, line + d), lambda n: [place(n, ones[k])])
+    for k in range(STEPS):
+        line_step(ctab, pair, first[1] + k, lambda n, d: place(n, after_one[k + 1 + d]), lambda n: [place(n, twos[k])])
+    for k in range(STEPS):
+        line = first[2] + k
+        line_step(ctab, pair, line, lambda n, d: place(n, after_two[k + 1 + d]), lambda n: [result(n, line)])
+
+
+def fused_kernel(row_devices, col_devices, lines, tiles, cov, ew, nw, dlon, dlat, fwd, rtab, big, ctab, relay, one, two, pads, winds,
+                 wind_sem, load_sem, up_send, up_recv, down_send, down_recv, hop_send, hop_recv, z_send, z_recv):
     r, c = lax.axis_index("row"), lax.axis_index("col")
     rows = lines * NLON
     edges, middle = tile_order(tiles)
@@ -400,11 +461,17 @@
         return pltpu.make_async_remote_copy(relay.at[k], big.at[t, after, :], hop_send.at[k], down_recv.at[t],
                                             device_id={"row": detour["low"]}, device_id_type=MESH)
 
+    wind_copies = [pltpu.make_async_copy(ref, winds.at[k], wind_sem.at[k]) for k, ref in enumerate((ew, nw, dlon, dlat))]
+    for copy in wind_copies:
+        copy.start()
     for t in edges:
         load(t).start()
     pl.semaphore_wait(barrier, count)
 
-    for t in edges + middle:
+    odd = r % 2 == 1
+
+    def send_slow(t):
+        low = high = r < 0
         if t in carried:
             k = carried.index(t)
             low, high = r == detour["low"], r == detour["high"]
@@ -416,18 +483,34 @@
             @pl.when(high)
             def _():
                 down_first(k, t).start()
-        else:
-            low = high = r < 0
-
-        @pl.when(has_up & ~low)
+
+        @pl.when(odd & has_up & ~low)
         def _():
             up(t).start()
 
-        @pl.when(has_down & ~high)
+        @pl.when(~odd & has_down & ~high)
         def _():
             down(t).start()
+
+    def send_quick(t):
+        @pl.when(odd)
+        def _():
+            down(t).start()
+
+        @pl.when(~odd)
+        def _():
+            up(t).start()
+
+    for t in edges:
+        send_slow(t)
+    for t in edges:
+        send_quick(t)
+    for t in middle:
+        send_slow(t)
     for t in middle:
         load(t).start()
+    for t in middle:
+        send_quick(t)
 
     def relay_step(k):
         t = carried[k]
@@ -442,7 +525,9 @@
             down_first(k, t).wait_recv()
             down_second(k, t).start()
 
-    east_wind, north_wind, lon, lat = ew[...], nw[...], dlon[...], dlat[...]
+    for copy in wind_copies:
+        copy.wait()
+    east_wind, north_wind, lon, lat = (winds[k] for k in range(4))
     half_east, half_north = 0.5 * east_wind, 0.5 * north_wind
     made = [1.0 - 2.0 * lon - 2.0 * lat, lon - half_east, lon + half_east, lat - half_north, lat + half_north]
     grid_lines = lon.shape[0]
@@ -482,36 +567,8 @@
     def _():
         fwd[pl.ds(tiles + STEPS, STEPS)] = jnp.zeros((STEPS, rows, LANES), jnp.float32)
 
-    sub = lax.broadcasted_iota(jnp.int32, (SUBS, LANES), 0)
-
-    def line_step(pair, line, source, stores, keeps=()):
-        for g in range(NLON // SUBS):
-            at = g * SUBS
-            coef = [ctab[k, line - 1, pl.ds(at, SUBS), :] for k in range(5)]
-            for n in range(len(pair)):
-
-                def read(d, shift=0, count=SUBS):
-                    ref, base = source(n, d)
-                    return ref[pl.ds(pl.multiple_of(base, SUBS) + shift, count), :]
-
-                def write(place, value):
-                    ref, base = place
-                    ref[pl.ds(pl.multiple_of(base + at, SUBS), SUBS), :] = value
-
-                seen = {d: read(d, at) for d in (-1, 0, 1)}
-                east, west = read(0, at + 1), read(0, at - 1)
-                if g == NLON // SUBS - 1:
-                    east = jnp.where(sub == SUBS - 1, read(0, 0, 1), east)
-                if g == 0:
-                    west = jnp.where(sub == 0, read(0, NLON - 1, 1), west)
-                value = (coef[0] * seen[0] + coef[1] * east) + (coef[2] * west + coef[3] * seen[1]) + coef[4] * seen[-1]
-                for place in stores(n):
-                    write(place, value)
-                for d, place in keeps:
-                    write(place(n), seen[d])
-
     def in_big(pair, n, slot):
-        return big.at[pair[n]], PAD + slot * NLON
+        return line_of(big, pair, n, slot)
 
     def in_fwd(pair, n, line):
         return fwd.at[pair[n] + STEPS], (line - STEPS) * NLON
@@ -527,21 +584,21 @@
             return two.at[n], PAD + (line - 5) * NLON
 
         def step1(line, _):
-            line_step(pair, line, lambda n, d: in_big(pair, n, line + d), lambda n: [at_one(n, line)])
+            line_step(ctab, pair, line, lambda n, d: in_big(pair, n, line + d), lambda n: [at_one(n, line)])
             return 0
 
         def step2(line, keep):
             places = lambda n: [at_two(n, line)] + ([in_big(pair, n, kept_two[line])] if keep else [])
             keeps = [(d, functools.partial(lambda n, slot: in_big(pair, n, slot), slot=kept_one[line + d]))
                      for d in ((-1, 0) if line == 5 else (0, 1))] if keep and line in (5, lines) else []
-            line_step(pair, line, lambda n, d: at_one(n, line + d), places, keeps)
+            line_step(ctab, pair, line, lambda n, d: at_one(n, line + d), places, keeps)
 
         def step2_plain(line, _):
             step2(line, False)
             return 0
 
         def step3(line, _):
-            line_step(pair, line, lambda n, d: at_two(n, line + d), lambda n: [in_fwd(pair, n, line)])
+            line_step(ctab, pair, line, lambda n, d: at_two(n, line + d), lambda n: [in_fwd(pair, n, line)])
             return 0
 
         lax.fori_loop(4, lines + 2, step1, 0)
@@ -552,34 +609,9 @@
         step2(lines, True)
         lax.fori_loop(6, lines, step3, 0)
 
-    def outer_columns(pair, south):
-        ones = [("one", k) for k in range(STEPS)]
-        twos = [("two", k) for k in range(STEPS)]
-        if south:
-            first = [lines + 2, lines + 1, lines]
-            after_one = [("big", lines - 1), ("big", lines)] + ones
-            after_two = [("big", lines - 3), ("big", lines - 2)] + twos
-        else:
-            first = [1, 2, 3]
-            after_one = ones + [("big", 5), ("big", 6)]
-            after_two = twos + [("big", 7), ("big", 8)]
-
-        def place(n, where):
-            name, k = where
-            if name == "big":
-                return in_big(pair, n, k)
-            return (one if name == "one" else two).at[n], PAD + k * NLON
-
-        for k in range(STEPS):
-            line = first[0] + k
-            line_step(pair, line, lambda n, d: in_big(pair, n, line + d), lambda n: [place(n, ones[k])])
-        for k in range(STEPS):
-            line_step(pair, first[1] + k, lambda n, d: place(n, after_one[k + 1 + d]), lambda n: [place(n, twos[k])])
-        for k in range(STEPS):
-            line = first[2] + k
-            line_step(pair, line, lambda n, d: place(n, after_two[k + 1 + d]), lambda n: [in_fwd(pair, n, line)])
-
-    odd = r % 2 == 1
+    def outer(pair, south):
+        outer_columns(big, ctab, one, two, lines, pair, south, lambda n, line: in_fwd(pair, n, line))
+
     quick, slow = odd_rows(odd, rows)
 
     def quick_columns(pair):
@@ -587,30 +619,35 @@
         def _():
             for t in pair:
                 up(t).wait_recv()
-            outer_columns(pair, False)
+            outer(pair, False)
 
         @pl.when(~odd)
         def _():
             for t in pair:
                 down(t).wait_recv()
-            outer_columns(pair, True)
+            outer(pair, True)
+
+    def slow_arrive(pair):
+        @pl.when(odd & has_up)
+        def _():
+            for t in pair:
+                down(t).wait_recv()
+
+        @pl.when(~odd & has_down)
+        def _():
+            for t in pair:
+                up(t).wait_recv()
 
     def slow_columns(pair):
+        slow_arrive(pair)
+
         @pl.when(odd)
         def _():
-            @pl.when(has_up)
-            def _():
-                for t in pair:
-                    down(t).wait_recv()
-            outer_columns(pair, True)
+            outer(pair, True)
 
         @pl.when(~odd)
         def _():
-            @pl.when(has_down)
-            def _():
-                for t in pair:
-                    up(t).wait_recv()
-            outer_columns(pair, False)
+            outer(pair, False)
 
     pieces = (rows - 2 * HALO) // PIECE
     side = HALO // PIECE
@@ -679,12 +716,15 @@
 
     lax.fori_loop(0, all_pairs, early, 0)
 
+    def held(tile, at):
+        return fwd[tile + STEPS, pl.ds(at, RBLOCK), :]
+
     def keep(tile, at, value):
         fwd[tile, pl.ds(at, RBLOCK), :] = value
 
     def ready_rows(part, _):
         z_wait(part, 0)
-        row_pass(fwd, rtab, 0, tiles, piece_start(part), PIECE, keep)
+        row_pass(held, rtab, 0, tiles, piece_start(part), PIECE, keep)
         return 0
 
     groups = slow_groups(all_pairs - edge_pairs)
@@ -710,11 +750,12 @@
             def _():
                 if n == 0:
                     lax.fori_loop(pieces + side, pieces + 2 * side, z_wait, 0)
-                row_pass(fwd, rtab, done, upto, slow, HALO, keep)
+                row_pass(held, rtab, done, upto, slow, HALO, keep)
             done = upto
         return 0
 
-    lax.fori_loop(0, all_pairs, late, 0)
+    lax.fori_loop(0, all_pairs - 1, late, 0)
+    slow_arrive(pair_of(all_pairs - 1))
 
     def sent(t, _):
         @pl.when(has_up)
@@ -754,14 +795,14 @@
     return jnp.where(odd, 0, rows - HALO), jnp.where(odd, rows - HALO, 0)
 
 
-def row_pass(fwd, rtab, a, b, start, count, store):
+def row_pass(read, rtab, a, b, start, count, store):
     edge = STEPS - 1
 
     def block(i, _):
         at = pl.multiple_of(start + i * RBLOCK, RBLOCK)
         got = {}
         for tile in range(a - STEPS, b + STEPS):
-            got[0, tile] = fwd[tile + STEPS, pl.ds(at, RBLOCK), :]
+            got[0, tile] = read(tile, at)
             for step in range(1, STEPS + 1):
                 mid = tile - step
                 if mid < a - STEPS + step:
@@ -783,10 +824,12 @@
     lax.fori_loop(0, count // RBLOCK, block, 0)
 
 
-def finish_kernel(tiles, fwd, rtab, out, last, done_sem, slow_sem):
+def finish_kernel(tiles, fwd, rtab, big, ctab, out, last, ends, one, two, done_sem, slow_sem):
     rows = out.shape[0]
+    lines = rows // NLON
     begin = rest(tiles)
-    quick, slow = odd_rows(lax.axis_index("row") % 2 == 1, rows)
+    odd = lax.axis_index("row") % 2 == 1
+    quick, slow = odd_rows(odd, rows)
     ready = pl.ds(pl.multiple_of(jnp.where(quick == 0, 0, HALO), SUBS), rows - HALO)
     late = pl.ds(pl.multiple_of(slow, SUBS), HALO)
 
@@ -798,14 +841,29 @@
     for copy in copies:
         copy.start()
 
+    pair = [tiles - STEPS - PAIR + n for n in range(PAIR)]
+
+    @pl.when(odd)
+    def _():
+        outer_columns(big, ctab, one, two, lines, pair, True, lambda n, line: (ends.at[n], (line - lines) * NLON))
+
+    @pl.when(~odd)
+    def _():
+        outer_columns(big, ctab, one, two, lines, pair, False, lambda n, line: (ends.at[n], (line - STEPS) * NLON))
+
+    def held(tile, at):
+        if tile in pair:
+            return ends[tile - pair[0], pl.ds(pl.multiple_of(at - slow, SUBS), RBLOCK), :]
+        return fwd[tile + STEPS, pl.ds(at, RBLOCK), :]
+
     def keep(tile, at, value):
         last[tile - begin, pl.ds(pl.multiple_of(at - slow, SUBS), RBLOCK), :] = value
 
-    row_pass(fwd, rtab, begin, tiles, slow, HALO, keep)
-    ends = [pltpu.make_async_copy(last.at[t - begin], out.at[late, lanes(t)], slow_sem.at[t]) for t in range(begin, tiles)]
-    for copy in ends:
+    row_pass(held, rtab, begin, tiles, slow, HALO, keep)
+    copies_left = [pltpu.make_async_copy(last.at[t - begin], out.at[late, lanes(t)], slow_sem.at[t]) for t in range(begin, tiles)]
+    for copy in copies_left:
         copy.start()
-    for copy in copies + ends:
+    for copy in copies + copies_left:
         copy.wait()
 
 
@@ -819,19 +877,24 @@
     detour = detours(row_devices, tiles)
     hops = len(detour["tiles"]) if detour else 1
     f32 = jnp.float32
-    held = (tiles + 2 * STEPS, rows, LANES)
-    room = 64 * 1024 * 1024 - 4 * held[0] * held[1] * held[2] - 1024 * 1024
-    fwd, rtab, _ = pl.pallas_call(
+    kept = [
+        (tiles + 2 * STEPS, rows, LANES),
+        (5, wide, LANES),
+        (tiles, 2 * PAD + 2 * HALO + rows, LANES),
+        (5, lines + 2 * edge, NLON, LANES),
+    ]
+    room = 64 * 1024 * 1024 - sum(4 * math.prod(shape) for shape in kept) - 1024 * 1024
+    made = pl.pallas_call(
         functools.partial(fused_kernel, row_devices, col_devices, lines, tiles),
-        in_specs=[pl.BlockSpec(memory_space=pl.ANY)] + [pl.BlockSpec(memory_space=pltpu.VMEM)] * 4,
-        out_specs=[pl.BlockSpec(memory_space=pltpu.VMEM)] * 2 + [pl.BlockSpec(memory_space=pl.ANY)],
-        out_shape=[pltpu.VMEM(held, f32), jax.ShapeDtypeStruct((5, wide, LANES), f32), jax.ShapeDtypeStruct((hops, HALO, LANES), f32)],
+        in_specs=[pl.BlockSpec(memory_space=pl.ANY)] * 5,
+        out_specs=[pl.BlockSpec(memory_space=pltpu.VMEM)] * len(kept) + [pl.BlockSpec(memory_space=pl.ANY)],
+        out_shape=[pltpu.VMEM(shape, f32) for shape in kept] + [jax.ShapeDtypeStruct((hops, HALO, LANES), f32)],
         scratch_shapes=[
-            pltpu.VMEM((tiles, 2 * PAD + 2 * HALO + rows, LANES), f32),
             pltpu.VMEM((PAIR, 2 * PAD + (lines - 2) * NLON, LANES), f32),
             pltpu.VMEM((PAIR, 2 * PAD + (lines - 4) * NLON, LANES), f32),
             pltpu.VMEM((5, slack, LANES), f32),
-            pltpu.VMEM((5, lines + 2 * edge, NLON, LANES), f32),
+            pltpu.VMEM((4,) + east_wind.shape, f32),
+            pltpu.SemaphoreType.DMA((4,)),
             pltpu.SemaphoreType.DMA((tiles,)),
             pltpu.SemaphoreType.DMA((tiles,)),
             pltpu.SemaphoreType.DMA((tiles,)),
@@ -846,16 +909,19 @@
     )(covariance, east_wind, north_wind, diffuse_lon, diffuse_lat)
     return pl.pallas_call(
         functools.partial(finish_kernel, tiles),
-        in_specs=[pl.BlockSpec(memory_space=pltpu.VMEM)] * 2,
+        in_specs=[pl.BlockSpec(memory_space=pltpu.VMEM)] * len(kept),
         out_specs=pl.BlockSpec(memory_space=pl.ANY),
         out_shape=jax.ShapeDtypeStruct((rows, cols), f32),
         scratch_shapes=[
             pltpu.VMEM((tiles - rest(tiles), HALO, LANES), f32),
+            pltpu.VMEM((PAIR, HALO, LANES), f32),
+            pltpu.VMEM((PAIR, 2 * PAD + HALO, LANES), f32),
+            pltpu.VMEM((PAIR, 2 * PAD + HALO, LANES), f32),
             pltpu.SemaphoreType.DMA((tiles,)),
             pltpu.SemaphoreType.DMA((tiles,)),
         ],
         compiler_params=pltpu.CompilerParams(vmem_limit_bytes=room),
-    )(pltpu.with_memory_space_constraint(fwd, pltpu.VMEM), rtab)
+    )(*[pltpu.with_memory_space_constraint(array, pltpu.VMEM) for array in made[: len(kept)]])
 
 
 def solution(mesh):

time: 92.6 us -> 89.7 us (0.969)
  Pallas kernels: 92.4 us -> 89.6 us
    pallas_call x1, Pallas kernels: 84.7 us -> 82.7 us  [fused_body(): pl.pallas_call(functools.partial(fused_kernel, row_devices, col_devices,...]
where the time goes in v3:
time: 89.7 us; the launch traced here: 89.6 us
  Pallas kernels  89.6 us (100%)
    pallas_call x1, Pallas kernels, fused_body(): pl.pallas_call(functools.partial(fused_kernel, row_devices, col_devices,...  82.7 us
    pallas_call x1, Pallas kernels, fused_body(): pl.pallas_call(functools.partial(finish_kernel, tiles), in_specs=[pl.Bloc...  6.87 us

profile of v3, /device:TPU:1, one launch (start us, length us, event | category | flops | bytes accessed | tf_op | source)
XLA Modules:
  0.0 89.6 jit_solution(11333112019050972674)
XLA Ops:
  0.0 82.7 %shard_map.55 = (f32[30,1536,128]{2,1,0:T(8,128)S(1)}, f32[5,32,128]{2,1,0:T(8,128)S(1)}, f32[24,2320,128]{2,1,0:T(8,128)S(1)}, f32[5,16,128,128]{3,2,1,0:T(8,128)S(1)}, f32[12,384,128]{2,1,0:T(8,128)}) custom-call(f32[1536,3072]{1,0:T(8,128)} %cov.1, f32[96,128]{1,0:T(8,128)} %ew.1, f32[96,128]{1,0:T(8,128)} %nw.1, f32[96,128]{1,0:T(8,128)} %dlon.1, ...), custom_call_target="tpu_custom_call" | custom-call | tf_op jit(solution)/shard_map/pallas_call | solution.py:887
  82.7 6.9 %shard_map.56 = f32[1536,3072]{1,0:T(8,128)} custom-call(f32[30,1536,128]{2,1,0:T(8,128)S(1)} %get-tuple-element.9.fwd, f32[5,32,128]{2,1,0:T(8,128)S(1)} %get-tuple-element.10.rtab, f32[24,2320,128]{2,1,0:T(8,128)S(1)} %get-tuple-element.11.big, f32[5,16,128,128]{3,2,1,0:T(8,128)S(1)} %get-tuple-element.12.ctab), custom_call_target="tpu_custom_call" | custom-call | tf_op jit(solution)/shard_map/pallas_call | solution.py:910

commit v4 on v3

--- a/solution.py
+++ b/solution.py
@@ -404,7 +404,7 @@
 
 
 def fused_kernel(row_devices, col_devices, lines, tiles, cov, ew, nw, dlon, dlat, fwd, rtab, big, ctab, relay, one, two, pads, winds,
-                 wind_sem, load_sem, up_send, up_recv, down_send, down_recv, hop_send, hop_recv, z_send, z_recv):
+                 wind_sem, load_sem, up_send, up_recv, down_send, down_recv, hop_send, hop_recv, z_send, z_recv, ready_sem):
     r, c = lax.axis_index("row"), lax.axis_index("col")
     rows = lines * NLON
     edges, middle = tile_order(tiles)
@@ -414,7 +414,6 @@
     has_right, has_left = c < col_devices - 1, c > 0
 
     partners = [(has_up, {"row": jnp.minimum(r + 1, row_devices - 1)}), (has_down, {"row": jnp.maximum(r - 1, 0)})]
-    partners += [(has_right, {"col": jnp.minimum(c + 1, col_devices - 1)}), (has_left, {"col": jnp.maximum(c - 1, 0)})]
     if detour:
         for a in (detour["low"], detour["high"]):
             for b in (detour["up_by"], detour["down_by"]):
@@ -460,6 +459,12 @@
     def down_second(k, t):
         return pltpu.make_async_remote_copy(relay.at[k], big.at[t, after, :], hop_send.at[k], down_recv.at[t],
                                             device_id={"row": detour["low"]}, device_id_type=MESH)
+
+    count = count + has_left.astype(jnp.int32)
+
+    @pl.when(has_right)
+    def _():
+        pl.semaphore_signal(barrier, inc=1, device_id={"col": jnp.minimum(c + 1, col_devices - 1)}, device_id_type=MESH)
 
     wind_copies = [pltpu.make_async_copy(ref, winds.at[k], wind_sem.at[k]) for k, ref in enumerate((ew, nw, dlon, dlat))]
     for copy in wind_copies:
@@ -511,6 +516,10 @@
         load(t).start()
     for t in middle:
         send_quick(t)
+
+    @pl.when(has_left)
+    def _():
+        pl.semaphore_signal(ready_sem, inc=1, device_id={"col": jnp.maximum(c - 1, 0)}, device_id_type=MESH)
 
     def relay_step(k):
         t = carried[k]
@@ -705,6 +714,10 @@
 
         @pl.when(i == edge_pairs - 1)
         def _():
+            @pl.when(has_right)
+            def _():
+                pl.semaphore_wait(ready_sem, 1)
+
             lax.fori_loop(0, pieces + side, z_start, 0)
 
         if detour:
@@ -754,9 +767,6 @@
             done = upto
         return 0
 
-    lax.fori_loop(0, all_pairs - 1, late, 0)
-    slow_arrive(pair_of(all_pairs - 1))
-
     def sent(t, _):
         @pl.when(has_up)
         def _():
@@ -767,7 +777,7 @@
             down(t).wait_send()
         return 0
 
-    lax.fori_loop(0, tiles, sent, 0)
+    lax.fori_loop(0, all_pairs - 1, late, 0)
     for k, t in enumerate(carried):
         @pl.when(r == detour["up_by"])
         def _():
@@ -776,6 +786,11 @@
         @pl.when(r == detour["down_by"])
         def _():
             down_second(k, t).wait_send()
+    final = tiles - STEPS - PAIR
+    lax.fori_loop(0, final, sent, 0)
+    lax.fori_loop(final + PAIR, tiles, sent, 0)
+    slow_arrive([final + n for n in range(PAIR)])
+    lax.fori_loop(final, final + PAIR, sent, 0)
 
 
 def slow_groups(pairs):
@@ -904,6 +919,7 @@
             pltpu.SemaphoreType.DMA((hops,)),
             pltpu.SemaphoreType.DMA((2 * rows // PIECE,)),
             pltpu.SemaphoreType.DMA((2 * rows // PIECE,)),
+            pltpu.SemaphoreType.REGULAR,
         ],
         compiler_params=pltpu.CompilerParams(collective_id=0, has_side_effects=True, vmem_limit_bytes=room),
     )(covariance, east_wind, north_wind, diffuse_lon, diffuse_lat)

time: 89.7 us -> 88.6 us (0.988)
  Pallas kernels: 89.6 us -> 88.5 us
    pallas_call x1, Pallas kernels: 82.7 us -> 81.6 us  [fused_body(): pl.pallas_call(functools.partial(fused_kernel, row_devices, col_devices,...]
where the time goes in v4:
time: 88.6 us; the launch traced here: 88.5 us
  Pallas kernels  88.5 us (100%)
    pallas_call x1, Pallas kernels, fused_body(): pl.pallas_call(functools.partial(fused_kernel, row_devices, col_devices,...  81.6 us
    pallas_call x1, Pallas kernels, fused_body(): pl.pallas_call(functools.partial(finish_kernel, tiles), in_specs=[pl.Bloc...  6.87 us

profile of v4, /device:TPU:1, one launch (start us, length us, event | category | flops | bytes accessed | tf_op | source)
XLA Modules:
  0.0 88.5 jit_solution(14166722647398079846)
XLA Ops:
  0.0 81.6 %shard_map.55 = (f32[30,1536,128]{2,1,0:T(8,128)S(1)}, f32[5,32,128]{2,1,0:T(8,128)S(1)}, f32[24,2320,128]{2,1,0:T(8,128)S(1)}, f32[5,16,128,128]{3,2,1,0:T(8,128)S(1)}, f32[12,384,128]{2,1,0:T(8,128)}) custom-call(f32[1536,3072]{1,0:T(8,128)} %cov.1, f32[96,128]{1,0:T(8,128)} %ew.1, f32[96,128]{1,0:T(8,128)} %nw.1, f32[96,128]{1,0:T(8,128)} %dlon.1, ...), custom_call_target="tpu_custom_call" | custom-call | tf_op jit(solution)/shard_map/pallas_call | solution.py:902
  81.6 6.9 %shard_map.56 = f32[1536,3072]{1,0:T(8,128)} custom-call(f32[30,1536,128]{2,1,0:T(8,128)S(1)} %get-tuple-element.9.fwd, f32[5,32,128]{2,1,0:T(8,128)S(1)} %get-tuple-element.10.rtab, f32[24,2320,128]{2,1,0:T(8,128)S(1)} %get-tuple-element.11.big, f32[5,16,128,128]{3,2,1,0:T(8,128)S(1)} %get-tuple-element.12.ctab), custom_call_target="tpu_custom_call" | custom-call | tf_op jit(solution)/shard_map/pallas_call | solution.py:926

commit v5 on v4

--- a/solution.py
+++ b/solution.py
@@ -467,10 +467,6 @@
         pl.semaphore_signal(barrier, inc=1, device_id={"col": jnp.minimum(c + 1, col_devices - 1)}, device_id_type=MESH)
 
     wind_copies = [pltpu.make_async_copy(ref, winds.at[k], wind_sem.at[k]) for k, ref in enumerate((ew, nw, dlon, dlat))]
-    for copy in wind_copies:
-        copy.start()
-    for t in edges:
-        load(t).start()
     pl.semaphore_wait(barrier, count)
 
     odd = r % 2 == 1
@@ -508,7 +504,10 @@
 
     for t in edges:
         send_slow(t)
+    for copy in wind_copies:
+        copy.start()
     for t in edges:
+        load(t).start()
         send_quick(t)
     for t in middle:
         send_slow(t)

time: 88.6 us -> 88.5 us (level)
  no operation moved by 1% of the time
where the time goes in v5:
time: 88.5 us; the launch traced here: 88.4 us
  Pallas kernels  88.4 us (100%)
    pallas_call x1, Pallas kernels, fused_body(): pl.pallas_call(functools.partial(fused_kernel, row_devices, col_devices,...  81.5 us
    pallas_call x1, Pallas kernels, fused_body(): pl.pallas_call(functools.partial(finish_kernel, tiles), in_specs=[pl.Bloc...  6.87 us

profile of v5, /device:TPU:1, one launch (start us, length us, event | category | flops | bytes accessed | tf_op | source)
XLA Modules:
  0.0 88.4 jit_solution(17511508897424885529)
XLA Ops:
  0.0 81.5 %shard_map.55 = (f32[30,1536,128]{2,1,0:T(8,128)S(1)}, f32[5,32,128]{2,1,0:T(8,128)S(1)}, f32[24,2320,128]{2,1,0:T(8,128)S(1)}, f32[5,16,128,128]{3,2,1,0:T(8,128)S(1)}, f32[12,384,128]{2,1,0:T(8,128)}) custom-call(f32[1536,3072]{1,0:T(8,128)} %cov.1, f32[96,128]{1,0:T(8,128)} %ew.1, f32[96,128]{1,0:T(8,128)} %nw.1, f32[96,128]{1,0:T(8,128)} %dlon.1, ...), custom_call_target="tpu_custom_call" | custom-call | tf_op jit(solution)/shard_map/pallas_call | solution.py:901
  81.5 6.9 %shard_map.56 = f32[1536,3072]{1,0:T(8,128)} custom-call(f32[30,1536,128]{2,1,0:T(8,128)S(1)} %get-tuple-element.9.fwd, f32[5,32,128]{2,1,0:T(8,128)S(1)} %get-tuple-element.10.rtab, f32[24,2320,128]{2,1,0:T(8,128)S(1)} %get-tuple-element.11.big, f32[5,16,128,128]{3,2,1,0:T(8,128)S(1)} %get-tuple-element.12.ctab), custom_call_target="tpu_custom_call" | custom-call | tf_op jit(solution)/shard_map/pallas_call | solution.py:925

commit v6 on v5

--- a/solution.py
+++ b/solution.py
@@ -850,8 +850,8 @@
     def lanes(t):
         return pl.ds(t * LANES, LANES)
 
-    copies = [pltpu.make_async_copy(fwd.at[t, ready, :], out.at[ready, lanes(t)], done_sem.at[t]) for t in range(tiles)]
-    copies += [pltpu.make_async_copy(fwd.at[t, late, :], out.at[late, lanes(t)], slow_sem.at[t]) for t in range(begin)]
+    copies = [pltpu.make_async_copy(fwd.at[t], out.at[:, lanes(t)], done_sem.at[t]) for t in range(begin)]
+    copies += [pltpu.make_async_copy(fwd.at[t, ready, :], out.at[ready, lanes(t)], done_sem.at[t]) for t in range(begin, tiles)]
     for copy in copies:
         copy.start()
 

time: 88.5 us -> 88.5 us (level)
  no operation moved by 1% of the time
where the time goes in v6:
time: 88.5 us; the launch traced here: 88.4 us
  Pallas kernels  88.4 us (100%)
    pallas_call x1, Pallas kernels, fused_body(): pl.pallas_call(functools.partial(fused_kernel, row_devices, col_devices,...  81.5 us
    pallas_call x1, Pallas kernels, fused_body(): pl.pallas_call(functools.partial(finish_kernel, tiles), in_specs=[pl.Bloc...  6.86 us

profile of v6, /device:TPU:1, one launch (start us, length us, event | category | flops | bytes accessed | tf_op | source)
XLA Modules:
  0.0 88.4 jit_solution(3110982978678136818)
XLA Ops:
  0.0 81.5 %shard_map.55 = (f32[30,1536,128]{2,1,0:T(8,128)S(1)}, f32[5,32,128]{2,1,0:T(8,128)S(1)}, f32[24,2320,128]{2,1,0:T(8,128)S(1)}, f32[5,16,128,128]{3,2,1,0:T(8,128)S(1)}, f32[12,384,128]{2,1,0:T(8,128)}) custom-call(f32[1536,3072]{1,0:T(8,128)} %cov.1, f32[96,128]{1,0:T(8,128)} %ew.1, f32[96,128]{1,0:T(8,128)} %nw.1, f32[96,128]{1,0:T(8,128)} %dlon.1, ...), custom_call_target="tpu_custom_call" | custom-call | tf_op jit(solution)/shard_map/pallas_call | solution.py:901
  81.5 6.9 %shard_map.56 = f32[1536,3072]{1,0:T(8,128)} custom-call(f32[30,1536,128]{2,1,0:T(8,128)S(1)} %get-tuple-element.9.fwd, f32[5,32,128]{2,1,0:T(8,128)S(1)} %get-tuple-element.10.rtab, f32[24,2320,128]{2,1,0:T(8,128)S(1)} %get-tuple-element.11.big, f32[5,16,128,128]{3,2,1,0:T(8,128)S(1)} %get-tuple-element.12.ctab), custom_call_target="tpu_custom_call" | custom-call | tf_op jit(solution)/shard_map/pallas_call | solution.py:925
